TPU v7x, 32 devices: a whole 2x2x4 slice. The times are simulated.
32 devices in a mesh: gx: 2 (over x), gy: 4 (over y, core), ha: 4 (over z).
Axes of the slice: x: 2, y: 2, z: 4, core: 2. Of those that a mesh axis runs over, the one named last changes fastest.
Arguments:
- tokens: bfloat16 [16, 64, 16, 384], P('gx', 'gy'), may hold values from -30 to 30
- input_weight: bfloat16 [384, 768], P(None, 'ha'), may hold values from -1 to 1
- output_weight: bfloat16 [256, 384], P('ha'), may hold values from -0.375 to 0.375
- tissue_bits: int32 [16, 64], P('gx', 'gy'), may hold values from 0 to 65535
- cotangent: bfloat16 [16, 64, 16, 384], P('gx', 'gy'), may hold values from -6 to 6
Outputs:
- token_gradient: bfloat16 [16, 64, 16, 384], P('gx', 'gy', None, 'ha')
- input_gradient: float32 [384, 768], P(None, 'ha')
- output_gradient: float32 [256, 384], P('ha')
All inputs are finite; a program needn't handle non-finite values.
Results may differ from a plain program's by a relative error of at most 0.018.
The roundings to bfloat16 on the way count: a program that leaves them out, or rounds other values in their place, can miss the bound.
Values may be sent and summed in bfloat16 or wider, within the bound.
A program may use at most 128 MiB of HBM per device.

v0:
```python
import jax
import jax.numpy as jnp
from jax import lax
from jax.sharding import PartitionSpec as P

HD = 64
REACH = 3


def extended(block, sides, width):
    for axis, dim in sides:
        count = lax.axis_size(axis)
        forward = [(i, i + 1) for i in range(count - 1)]
        backward = [(target, source) for source, target in forward]
        low = lax.ppermute(
            lax.slice_in_dim(block, block.shape[dim] - width, None, axis=dim), axis, forward
        )
        high = lax.ppermute(lax.slice_in_dim(block, 0, width, axis=dim), axis, backward)
        block = jnp.concatenate([low, block, high], axis=dim)
    return block


def block_length(extent, plane_rows):
    for length in range(1, extent + 1):
        if extent % length == 0 and length * plane_rows >= 512:
            return length
    return extent


def shards(tokens, input_weight, output_weight, tissue_bits, cotangent):
    width_x, width_y, depth, model_width = tokens.shape
    local_heads = output_weight.shape[0] // HD
    token_count = width_x * width_y * depth
    score_scale = HD ** (-0.5)
    flat_tokens = tokens.reshape(token_count, model_width)
    flat_cotangent = cotangent.reshape(token_count, model_width)
    bit_values = 2 ** jnp.arange(depth, dtype=jnp.int32)
    key_valid = (tissue_bits[:, :, None] // bit_values % 2).astype(jnp.bfloat16)
    key_span_x_full = width_x + 2 * REACH
    key_span_y = width_y + 2 * REACH
    projected = jnp.dot(flat_tokens, input_weight, preferred_element_type=jnp.float32).astype(
        jnp.bfloat16
    )
    projected = projected.reshape(token_count, local_heads, 3, HD)
    queries = projected[:, :, 0, :].reshape(token_count, local_heads * HD)
    pair_local = projected[:, :, 1:, :].reshape(width_x, width_y, depth, local_heads * 2 * HD)
    pair_padded, valid_padded = (
        extended(pair_local, (("gx", 0), ("gy", 1)), REACH),
        extended(key_valid, (("gx", 0), ("gy", 1)), REACH),
    )
    upstream = jnp.einsum(
        "nd,ed->ne", flat_cotangent, output_weight, preferred_element_type=jnp.float32
    ).astype(jnp.bfloat16)
    block_x = block_length(width_x, width_y * depth)
    block_count = width_x // block_x
    key_span_x = block_x + 2 * REACH
    query_rows = block_x * width_y * depth
    key_rows = key_span_x * key_span_y * depth
    query_slots = jnp.arange(query_rows)
    query_x = query_slots // (width_y * depth)
    query_y = query_slots // depth % width_y
    query_z = query_slots % depth
    key_slots = jnp.arange(key_rows)
    key_x = key_slots // (key_span_y * depth) - REACH
    key_y = key_slots // depth % key_span_y - REACH
    key_z = key_slots % depth
    within = (
        (jnp.abs(query_x[:, None] - key_x[None, :]) <= REACH)
        & (jnp.abs(query_y[:, None] - key_y[None, :]) <= REACH)
        & (jnp.abs(query_z[:, None] - key_z[None, :]) <= REACH)
    )
    self_pair = (
        (query_x[:, None] == key_x[None, :])
        & (query_y[:, None] == key_y[None, :])
        & (query_z[:, None] == key_z[None, :])
    )
    query_grid = queries.reshape(width_x, width_y, depth, local_heads, HD)
    upstream_grid = upstream.reshape(width_x, width_y, depth, local_heads, HD)
    pair_grid = pair_padded.reshape(key_span_x_full, key_span_y, depth, local_heads, 2, HD)

    def attend_block(block_index, carry):
        query_sums, pair_sums, outputs = carry
        first_row = block_index * block_x
        query_block = lax.dynamic_slice_in_dim(query_grid, first_row, block_x, 0).reshape(
            query_rows, local_heads, HD
        )
        upstream_block = lax.dynamic_slice_in_dim(upstream_grid, first_row, block_x, 0).reshape(
            query_rows, local_heads, HD
        )
        pair_block = lax.dynamic_slice_in_dim(pair_grid, first_row, key_span_x, 0).reshape(
            key_rows, local_heads, 2, HD
        )
        keys_block = pair_block[:, :, 0, :]
        values_block = pair_block[:, :, 1, :]
        live_keys = (
            lax.dynamic_slice_in_dim(valid_padded, first_row, key_span_x, 0).reshape(key_rows) > 0
        )
        allowed = within & (live_keys[None, :] | self_pair)
        scores = (
            jnp.einsum("qhe,khe->hqk", query_block, keys_block, preferred_element_type=jnp.float32)
            * score_scale
        )
        scores = jnp.where(allowed[None], scores, -jnp.inf)
        row_max = jnp.max(scores, axis=-1, keepdims=True)
        raised = jnp.exp(scores - row_max)
        weights = (raised / jnp.sum(raised, axis=-1, keepdims=True)).astype(jnp.bfloat16)
        result = jnp.einsum(
            "hqk,khe->qhe", weights, values_block, preferred_element_type=jnp.float32
        )
        weight_gradient = jnp.einsum(
            "qhe,khe->hqk", upstream_block, values_block, preferred_element_type=jnp.float32
        )
        row_inner = jnp.sum(upstream_block.astype(jnp.float32) * result, axis=-1)
        score_gradient = (
            weights.astype(jnp.float32) * (weight_gradient - row_inner.T[:, :, None]) * score_scale
        ).astype(jnp.bfloat16)
        query_gradient = jnp.einsum(
            "hqk,khe->qhe", score_gradient, keys_block, preferred_element_type=jnp.float32
        )
        key_gradient = jnp.einsum(
            "hqk,qhe->khe", score_gradient, query_block, preferred_element_type=jnp.float32
        )
        value_gradient = jnp.einsum(
            "hqk,qhe->khe", weights, upstream_block, preferred_element_type=jnp.float32
        )
        pair_gradient = jnp.stack([key_gradient, value_gradient], axis=2).reshape(
            key_span_x, key_span_y, depth, local_heads * 2 * HD
        )
        query_sums = lax.dynamic_update_slice_in_dim(
            query_sums,
            query_gradient.reshape(block_x, width_y, depth, local_heads * HD),
            first_row,
            0,
        )
        previous = lax.dynamic_slice_in_dim(pair_sums, first_row, key_span_x, 0)
        pair_sums = lax.dynamic_update_slice_in_dim(
            pair_sums, previous + pair_gradient, first_row, 0
        )
        outputs = lax.dynamic_update_slice_in_dim(
            outputs,
            result.astype(jnp.bfloat16).reshape(block_x, width_y, depth, local_heads * HD),
            first_row,
            0,
        )
        return (query_sums, pair_sums, outputs)

    start = (
        jnp.zeros((width_x, width_y, depth, local_heads * HD), jnp.float32),
        jnp.zeros((key_span_x_full, key_span_y, depth, local_heads * 2 * HD), jnp.float32),
        jnp.zeros((width_x, width_y, depth, local_heads * HD), jnp.bfloat16),
    )
    query_sums, pair_sums, outputs = lax.fori_loop(0, block_count, attend_block, start)
    rims_first = jnp.concatenate([pair_sums[:REACH], pair_sums[width_x + REACH :]], axis=0)
    from_first = extended(rims_first.astype(jnp.bfloat16), (("gx", 0),), REACH).astype(
        rims_first.dtype
    )
    interior = pair_sums[REACH : width_x + REACH]
    interior = interior.at[:REACH].add(from_first[:REACH])
    interior = interior.at[width_x - REACH :].add(from_first[3 * REACH :])
    rims_second = jnp.concatenate([interior[:, :REACH], interior[:, width_y + REACH :]], axis=1)
    from_second = extended(rims_second.astype(jnp.bfloat16), (("gy", 1),), REACH).astype(
        rims_second.dtype
    )
    centre = interior[:, REACH : width_y + REACH]
    centre = centre.at[:, :REACH].add(from_second[:, :REACH])
    centre = centre.at[:, width_y - REACH :].add(from_second[:, 3 * REACH :])
    query_part = query_sums.reshape(token_count, local_heads, 1, HD)
    pair_part = centre.reshape(token_count, local_heads, 2, HD)
    dprojected = (
        jnp.concatenate([query_part, pair_part], axis=2)
        .reshape(token_count, local_heads * 3 * HD)
        .astype(jnp.bfloat16)
    )
    all_heads = lax.all_gather(dprojected, "ha", axis=1, tiled=True)
    all_columns = lax.all_to_all(input_weight, "ha", split_axis=0, concat_axis=1, tiled=True)
    share = all_columns.shape[0]
    summed = jnp.einsum("nc,dc->nd", all_heads, all_columns, preferred_element_type=jnp.float32)
    token_gradient = summed.reshape(width_x, width_y, depth, share).astype(jnp.bfloat16)
    attended_flat = outputs.reshape(token_count, local_heads * HD)
    part_input = jnp.einsum(
        "nd,nc->dc", flat_tokens, dprojected, preferred_element_type=jnp.float32
    )
    part_output = jnp.einsum(
        "ne,nd->ed", attended_flat, flat_cotangent, preferred_element_type=jnp.float32
    )
    summed_input, summed_output = (
        lax.psum(part_input.astype(jnp.bfloat16), ("gx", "gy")).astype(jnp.float32),
        lax.psum(part_output.astype(jnp.bfloat16), ("gx", "gy")).astype(jnp.float32),
    )
    normaliser = (token_count * lax.axis_size("gx") * lax.axis_size("gy")) ** (-0.5)
    return (token_gradient, summed_input * normaliser, summed_output * normaliser)


def solution(mesh):
    placed = (
        P("gx", "gy", None, None),
        P(None, "ha"),
        P("ha", None),
        P("gx", "gy"),
        P("gx", "gy", None, None),
    )
    return jax.shard_map(
        shards,
        mesh=mesh,
        in_specs=placed,
        out_specs=(P("gx", "gy", None, "ha"), P(None, "ha"), P("ha", None)),
        check_vma=False,
    )
```

profile of v0, /device:TPU:9, one launch (start us, length us, event | category | flops | bytes accessed | tf_op | source)
XLA Modules:
  0.0 319.4 jit_solution(4277099670468060898)
XLA Ops:
  11.0 3.1 collective-permute-start.4
  21.0 5.2 %collective-permute-start = (bf16[3,16,16,128]{3,2,1,0:T(8,128)(2,1)}, bf16[3,16,16,128]{3,2,1,0:T(8,128)(2,1)}, u32[]{:S(2)}, u32[]{:S(2)}) collective-permute-start(bf16[3,16,16,128]{3,2,1,0:T(8,128)(2,1)} %slice.209), channel_id=1, source_target_pairs={{0,16},{1,17},{2,18},{3,19},{4,20},{5,21},{6,22},{7,23},{8,24},{9,... | collective-permute-start | bytes 589832 | tf_op jit(solution)/shard_map/ppermute | solution.py:15
  34.8 4.5 %collective-permute-start.6 = (bf16[14,3,16]{2,1,0:T(4,128)(2,1)S(1)}, bf16[14,3,16]{2,1,0:T(4,128)(2,1)S(1)}, u32[]{:S(2)}, u32[]{:S(2)}) collective-permute-start(bf16[14,3,16]{2,1,0:T(4,128)(2,1)S(1)} %get-tuple-element.407), channel_id=1, source_target_pairs={{0,4},{4,8},{8,12},{1,5},{5,9},{9,13},{2,6},{6,10},{10,14},{3,7},{... | collective-permute-start | bytes 4040 | tf_op jit(solution)/shard_map/ppermute | solution.py:15
  44.2 3.6 %collective-permute-start.2 = (bf16[14,3,16,128]{3,2,1,0:T(8,128)(2,1)S(1)}, bf16[14,3,16,128]{3,2,1,0:T(8,128)(2,1)S(1)}, u32[]{:S(2)}, u32[]{:S(2)}) collective-permute-start(bf16[14,3,16,128]{3,2,1,0:T(8,128)(2,1)S(1)} %get-tuple-element.401), channel_id=1, source_target_pairs={{0,4},{4,8},{8,12},{1,5},{5,9},{9,13},{2,6},{6,10},{10,14},{3,7},{... | collective-permute-start | bytes 516104 | tf_op jit(solution)/shard_map/ppermute | solution.py:15
  47.9 1.9 collective-permute-start.3
  56.1 2.1 reshape.487
  61.8 145.0 %while.23 = (s32[]{:T(128)}, bf16[8,16,16,64]{3,2,1,0:T(8,128)(2,1)}, f32[14,22,16,128]{3,2,1,0:T(8,128)}, bf16[8,16,16,64]{3,2,1,0:T(8,128)(2,1)}, bf16[14,22,1...) while((s32[]{:T(128)}, ...), condition=%wide.region_4.5_spmd.clone.clone, body=%wide.region_0.4_spmd.clone.clone.sunk | while | flops 1152845056 | bytes 95118744 | solution.py:152
  61.8 2.5 constant_dynamic-slice_fusion.8
  66.5 5.8 %fusion.84 = (f32[512]{0:T(512)S(1)}, f32[512,2816]{1,0:T(8,128)S(1)}) fusion(bf16[512,64]{1,0:T(8,128)(2,1)S(1)} %bitcast.144, bf16[2816,1,2,64]{3,0,2,1:T(8,128)(2,1)S(1)} %bitcast.138, pred[2816]{0:T(1024)(128)(4,1)S(1)} %gt.22, s32[2816]{0:T(1024)S(1)} %get-tuple-element.564, s32[512]{0:T(512)S(1)} %get-tuple-element.565, ...), kind=kOutput, calls=%fused_computation.123.clone.1 | convolution fusion | flops 214826496 | bytes 6667264 | tf_op jit(solution)/shard_map/while/body/eval_jaxpr/qhe,khe->hqk/dot_general | solution.py:100
  73.2 3.0 divide_convert_fusion.2
  77.3 3.0 fusion.86
  84.2 4.6 %copy.78 = f32[2816,1,2,64]{3,2,0,1:T(2,128)} copy(f32[2816,1,2,64]{0,3,2,1:T(8,128)} %pad_maximum_fusion.13) | data formatting | bytes 2883584 | tf_op jit(solution)/shard_map/while/body/eval_jaxpr/stack | solution.py:126
  88.8 3.9 %reshape.515 = f32[8,22,16,128]{3,2,1,0:T(8,128)} reshape(f32[2816,1,2,64]{3,2,0,1:T(2,128)} %copy.78) | data formatting | bytes 2883584 | tf_op jit(solution)/shard_map/while/body/eval_jaxpr/reshape | solution.py:126
  92.7 3.3 %add_dynamic-update-slice_fusion.2 = f32[14,22,16,128]{3,2,1,0:T(8,128)} fusion(f32[14,22,16,128]{3,2,1,0:T(8,128)} %get-tuple-element.535, s32[]{:T(128)S(6)} %select_n.323, f32[8,22,16,128]{3,2,1,0:T(8,128)} %reshape.515), kind=kLoop, calls=%fused_computation.17.clone.1 | loop fusion | flops 360448 | bytes 4325380 | tf_op jit(solution)/shard_map/while/body/eval_jaxpr/dynamic_update_slice | solution.py:136
  98.1 2.5 constant_dynamic-slice_fusion.8
  102.7 5.8 %fusion.84 = (f32[512]{0:T(512)S(1)}, f32[512,2816]{1,0:T(8,128)S(1)}) fusion(bf16[512,64]{1,0:T(8,128)(2,1)S(1)} %bitcast.144, bf16[2816,1,2,64]{3,0,2,1:T(8,128)(2,1)S(1)} %bitcast.138, pred[2816]{0:T(1024)(128)(4,1)S(1)} %gt.22, s32[2816]{0:T(1024)S(1)} %get-tuple-element.564, s32[512]{0:T(512)S(1)} %get-tuple-element.565, ...), kind=kOutput, calls=%fused_computation.123.clone.1 | convolution fusion | flops 214826496 | bytes 6667264 | tf_op jit(solution)/shard_map/while/body/eval_jaxpr/qhe,khe->hqk/dot_general | solution.py:100
  109.4 3.0 divide_convert_fusion.2
  113.5 3.0 fusion.86
  120.4 4.6 %copy.78 = f32[2816,1,2,64]{3,2,0,1:T(2,128)} copy(f32[2816,1,2,64]{0,3,2,1:T(8,128)} %pad_maximum_fusion.13) | data formatting | bytes 2883584 | tf_op jit(solution)/shard_map/while/body/eval_jaxpr/stack | solution.py:126
  125.0 3.9 %reshape.515 = f32[8,22,16,128]{3,2,1,0:T(8,128)} reshape(f32[2816,1,2,64]{3,2,0,1:T(2,128)} %copy.78) | data formatting | bytes 2883584 | tf_op jit(solution)/shard_map/while/body/eval_jaxpr/reshape | solution.py:126
  128.9 3.2 %add_dynamic-update-slice_fusion.2 = f32[14,22,16,128]{3,2,1,0:T(8,128)} fusion(f32[14,22,16,128]{3,2,1,0:T(8,128)} %get-tuple-element.535, s32[]{:T(128)S(6)} %select_n.323, f32[8,22,16,128]{3,2,1,0:T(8,128)} %reshape.515), kind=kLoop, calls=%fused_computation.17.clone.1 | loop fusion | flops 360448 | bytes 4325380 | tf_op jit(solution)/shard_map/while/body/eval_jaxpr/dynamic_update_slice | solution.py:136
  134.2 2.5 constant_dynamic-slice_fusion.8
  138.9 5.8 %fusion.84 = (f32[512]{0:T(512)S(1)}, f32[512,2816]{1,0:T(8,128)S(1)}) fusion(bf16[512,64]{1,0:T(8,128)(2,1)S(1)} %bitcast.144, bf16[2816,1,2,64]{3,0,2,1:T(8,128)(2,1)S(1)} %bitcast.138, pred[2816]{0:T(1024)(128)(4,1)S(1)} %gt.22, s32[2816]{0:T(1024)S(1)} %get-tuple-element.564, s32[512]{0:T(512)S(1)} %get-tuple-element.565, ...), kind=kOutput, calls=%fused_computation.123.clone.1 | convolution fusion | flops 214826496 | bytes 6667264 | tf_op jit(solution)/shard_map/while/body/eval_jaxpr/qhe,khe->hqk/dot_general | solution.py:100
  145.6 3.0 divide_convert_fusion.2
  149.7 3.0 fusion.86
  156.6 4.6 %copy.78 = f32[2816,1,2,64]{3,2,0,1:T(2,128)} copy(f32[2816,1,2,64]{0,3,2,1:T(8,128)} %pad_maximum_fusion.13) | data formatting | bytes 2883584 | tf_op jit(solution)/shard_map/while/body/eval_jaxpr/stack | solution.py:126
  161.2 3.9 %reshape.515 = f32[8,22,16,128]{3,2,1,0:T(8,128)} reshape(f32[2816,1,2,64]{3,2,0,1:T(2,128)} %copy.78) | data formatting | bytes 2883584 | tf_op jit(solution)/shard_map/while/body/eval_jaxpr/reshape | solution.py:126
  165.1 3.3 %add_dynamic-update-slice_fusion.2 = f32[14,22,16,128]{3,2,1,0:T(8,128)} fusion(f32[14,22,16,128]{3,2,1,0:T(8,128)} %get-tuple-element.535, s32[]{:T(128)S(6)} %select_n.323, f32[8,22,16,128]{3,2,1,0:T(8,128)} %reshape.515), kind=kLoop, calls=%fused_computation.17.clone.1 | loop fusion | flops 360448 | bytes 4325380 | tf_op jit(solution)/shard_map/while/body/eval_jaxpr/dynamic_update_slice | solution.py:136
  170.5 2.5 constant_dynamic-slice_fusion.8
  175.1 5.8 %fusion.84 = (f32[512]{0:T(512)S(1)}, f32[512,2816]{1,0:T(8,128)S(1)}) fusion(bf16[512,64]{1,0:T(8,128)(2,1)S(1)} %bitcast.144, bf16[2816,1,2,64]{3,0,2,1:T(8,128)(2,1)S(1)} %bitcast.138, pred[2816]{0:T(1024)(128)(4,1)S(1)} %gt.22, s32[2816]{0:T(1024)S(1)} %get-tuple-element.564, s32[512]{0:T(512)S(1)} %get-tuple-element.565, ...), kind=kOutput, calls=%fused_computation.123.clone.1 | convolution fusion | flops 214826496 | bytes 6667264 | tf_op jit(solution)/shard_map/while/body/eval_jaxpr/qhe,khe->hqk/dot_general | solution.py:100
  181.8 3.0 divide_convert_fusion.2
  185.9 3.0 fusion.86
  192.8 4.6 %copy.78 = f32[2816,1,2,64]{3,2,0,1:T(2,128)} copy(f32[2816,1,2,64]{0,3,2,1:T(8,128)} %pad_maximum_fusion.13) | data formatting | bytes 2883584 | tf_op jit(solution)/shard_map/while/body/eval_jaxpr/stack | solution.py:126
  197.4 3.9 %reshape.515 = f32[8,22,16,128]{3,2,1,0:T(8,128)} reshape(f32[2816,1,2,64]{3,2,0,1:T(2,128)} %copy.78) | data formatting | bytes 2883584 | tf_op jit(solution)/shard_map/while/body/eval_jaxpr/reshape | solution.py:126
  201.3 3.2 %add_dynamic-update-slice_fusion.2 = f32[14,22,16,128]{3,2,1,0:T(8,128)} fusion(f32[14,22,16,128]{3,2,1,0:T(8,128)} %get-tuple-element.535, s32[]{:T(128)S(6)} %select_n.323, f32[8,22,16,128]{3,2,1,0:T(8,128)} %reshape.515), kind=kLoop, calls=%fused_computation.17.clone.1 | loop fusion | flops 360448 | bytes 4325380 | tf_op jit(solution)/shard_map/while/body/eval_jaxpr/dynamic_update_slice | solution.py:136
  206.8 2.0 convert.13
  208.9 4.9 %collective-permute-start.8 = (bf16[3,22,16,128]{3,2,1,0:T(8,128)(2,1)S(1)}, bf16[3,22,16,128]{3,2,1,0:T(8,128)(2,1)S(1)}, u32[]{:S(2)}, u32[]{:S(2)}) collective-permute-start(bf16[3,22,16,128]{3,2,1,0:T(8,128)(2,1)S(1)} %get-tuple-element.399), channel_id=1, source_target_pairs={{0,16},{1,17},{2,18},{3,19},{4,20},{5,21},{6,22},{7,23},{8,24},{9,... | collective-permute-start | bytes 811016 | tf_op jit(solution)/shard_map/ppermute | solution.py:15
  215.3 3.0 collective-permute-done.8
  218.3 4.1 %collective-permute-done.9 = bf16[3,22,16,128]{3,2,1,0:T(8,128)(2,1)S(1)} collective-permute-done((bf16[3,22,16,128]{3,2,1,0:T(8,128)(2,1)S(1)}, bf16[3,22,16,128]{3,2,1,0:T(8,128)(2,1)S(1)}, u32[]{:S(2)}, u32[]{:S(2)}) %collective-permute-start.9) | collective-permute-done | bytes 270368 | tf_op jit(solution)/shard_map/ppermute | solution.py:18
  223.4 4.3 %collective-permute-start.10 = (bf16[8,3,16,128]{3,2,1,0:T(8,128)(2,1)}, bf16[8,3,16,128]{3,2,1,0:T(8,128)(2,1)}, u32[]{:S(2)}, u32[]{:S(2)}) collective-permute-start(bf16[8,3,16,128]{3,2,1,0:T(8,128)(2,1)} %get-tuple-element.405), channel_id=1, source_target_pairs={{0,4},{4,8},{8,12},{1,5},{5,9},{9,13},{2,6},{6,10},{10,14},{3,7},{... | collective-permute-start | bytes 294920 | tf_op jit(solution)/shard_map/ppermute | solution.py:15
  231.7 2.3 collective-permute-done.11
  237.4 2.5 reshape.491
  242.7 9.4 %all_to_all.19 = bf16[4,96,192]{2,1,0:T(8,128)(2,1)S(1)} all-to-all(bf16[4,96,192]{2,1,0:T(8,128)(2,1)S(1)} %bitcast.159), channel_id=1, replica_groups=mesh['gx'=2,'gy'=4,'ha'=4] {'ha'}, dimensions={0} | all-to-all | bytes 294912 | tf_op jit(solution)/shard_map/all_to_all | solution.py:175
  254.3 20.4 %psum.15 = bf16[64,384]{1,0:T(8,128)(2,1)S(1)} all-reduce(bf16[64,384]{1,0:T(8,128)(2,1)S(1)} %fusion.9), channel_id=1, replica_groups=mesh['gx'=2,'gy'=4,'ha'=4] {'gx','gy'}, use_global_device_ids=true, to_apply=%region_6.7 | all-reduce | flops 24576 | bytes 98304 | tf_op jit(solution)/shard_map/psum | solution.py:188
  275.4 18.1 %all-reduce.2.cloned.1.call-done = bf16[384,192]{0,1:T(8,128)(2,1)} async-done(((bf16[384,192]{0,1:T(8,128)(2,1)}), bf16[384,192]{0,1:T(8,128)(2,1)}) %all-reduce.2.cloned.1.call-update) | async-done | bytes 147472 | tf_op jit(solution)/shard_map/psum | solution.py:187
  295.1 8.5 %all-gather.2.cloned.1.call-done = bf16[2048,768]{0,1:T(8,128)(2,1)} async-done(((bf16[2048,192]{0,1:T(8,128)(2,1)}), bf16[2048,768]{0,1:T(8,128)(2,1)}) %all-gather.2.cloned.1.call-update) | async-done | bytes 3145744 | tf_op jit(solution)/shard_map/all_gather | solution.py:174
  303.7 4.6 %copy.59 = bf16[2048,768]{1,0:T(8,128)(2,1)} copy(bf16[2048,768]{0,1:T(8,128)(2,1)} %all-gather.2.cloned.1.call-done) | data formatting | bytes 6291456 | tf_op jit(solution)/shard_map/all_gather | solution.py:174
  308.3 3.7 %convolution_convert_fusion.2 = bf16[8,16,16,96]{3,2,1,0:T(8,128)(2,1)} fusion(bf16[8,16,16,768]{3,2,1,0:T(8,128)(2,1)} %bitcast.148, bf16[96,768,1,1]{1,0,2,3:T(8,128)(2,1)S(1)} %reshape.511), kind=kOutput, calls=%fused_computation.33 | convolution fusion | flops 302186496 | bytes 3686400 | tf_op jit(solution)/shard_map/nc,dc->nd/dot_general | solution.py:177
  (262 shorter events, 89.6 us)
Async XLA Ops:
  8.0 7.4 %copy-start = (bf16[8,16,16,384]{3,2,1,0:T(8,128)(2,1)S(1)}, bf16[8,16,16,384]{3,2,1,0:T(8,128)(2,1)}, u32[]{:S(2)}) copy-start(bf16[8,16,16,384]{3,2,1,0:T(8,128)(2,1)} %param.15) | copy-start | bytes 4718596
  8.0 285.5 %all-reduce.2.cloned.1.call-start = ((), (), s32[]{:S(2)}) async-start(), calls=%async_computation.2 | async-start | bytes 294912 | tf_op jit(solution)/shard_map/psum | solution.py:187
  10.3 5.0 %copy-start.15 = (bf16[8,16,16]{2,1,0:T(8,128)(2,1)}, bf16[8,16,16]{2,1,0:T(8,128)(2,1)S(1)}, u32[]{:S(2)}) copy-start(bf16[8,16,16]{2,1,0:T(8,128)(2,1)S(1)} %fusion.16) | copy-start | bytes 12292
  11.0 23.0 %collective-permute-start.4 = (bf16[3,16,16]{2,1,0:T(8,128)(2,1)}, bf16[3,16,16]{2,1,0:T(8,128)(2,1)S(1)}, u32[]{:S(2)}, u32[]{:S(2)}) collective-permute-start(bf16[3,16,16]{2,1,0:T(8,128)(2,1)} %get-tuple-element.409), channel_id=1, source_target_pairs={{0,16},{1,17},{2,18},{3,19},{4,20},{5,21},{6,22},{7,23},{8,24},{9,... | collective-permute-start | bytes 4616 | tf_op jit(solution)/shard_map/ppermute | solution.py:15
  14.1 19.9 %collective-permute-start.5 = (bf16[3,16,16]{2,1,0:T(8,128)(2,1)}, bf16[3,16,16]{2,1,0:T(8,128)(2,1)}, u32[]{:S(2)}, u32[]{:S(2)}) collective-permute-start(bf16[3,16,16]{2,1,0:T(8,128)(2,1)} %get-tuple-element.410), channel_id=1, source_target_pairs={{16,0},{17,1},{18,2},{19,3},{20,4},{21,5},{22,6},{23,7},{24,8},{25... | collective-permute-start | bytes 4616 | tf_op jit(solution)/shard_map/ppermute | solution.py:18
  15.4 14.8 %copy-start.8 = (bf16[8,16,16,384]{3,2,1,0:T(8,128)(2,1)S(1)}, bf16[8,16,16,384]{3,2,1,0:T(8,128)(2,1)}, u32[]{:S(2)}) copy-start(bf16[8,16,16,384]{3,2,1,0:T(8,128)(2,1)} %param.19) | copy-start | bytes 4718596
  21.0 20.3 %collective-permute-start = (bf16[3,16,16,128]{3,2,1,0:T(8,128)(2,1)}, bf16[3,16,16,128]{3,2,1,0:T(8,128)(2,1)}, u32[]{:S(2)}, u32[]{:S(2)}) collective-permute-start(bf16[3,16,16,128]{3,2,1,0:T(8,128)(2,1)} %slice.209), channel_id=1, source_target_pairs={{0,16},{1,17},{2,18},{3,19},{4,20},{5,21},{6,22},{7,23},{8,24},{9,... | collective-permute-start | bytes 589832 | tf_op jit(solution)/shard_map/ppermute | solution.py:15
  28.3 14.0 %collective-permute-start.1 = (bf16[3,16,16,128]{3,2,1,0:T(8,128)(2,1)}, bf16[3,16,16,128]{3,2,1,0:T(8,128)(2,1)}, u32[]{:S(2)}, u32[]{:S(2)}) collective-permute-start(bf16[3,16,16,128]{3,2,1,0:T(8,128)(2,1)} %slice.212), channel_id=1, source_target_pairs={{16,0},{17,1},{18,2},{19,3},{20,4},{21,5},{22,6},{23,7},{24,8},{25... | collective-permute-start | bytes 589832 | tf_op jit(solution)/shard_map/ppermute | solution.py:18
  34.8 18.1 %collective-permute-start.6 = (bf16[14,3,16]{2,1,0:T(4,128)(2,1)S(1)}, bf16[14,3,16]{2,1,0:T(4,128)(2,1)S(1)}, u32[]{:S(2)}, u32[]{:S(2)}) collective-permute-start(bf16[14,3,16]{2,1,0:T(4,128)(2,1)S(1)} %get-tuple-element.407), channel_id=1, source_target_pairs={{0,4},{4,8},{8,12},{1,5},{5,9},{9,13},{2,6},{6,10},{10,14},{3,7},{... | collective-permute-start | bytes 4040 | tf_op jit(solution)/shard_map/ppermute | solution.py:15
  39.3 13.5 %collective-permute-start.7 = (bf16[14,3,16]{2,1,0:T(4,128)(2,1)S(1)}, bf16[14,3,16]{2,1,0:T(4,128)(2,1)S(1)}, u32[]{:S(2)}, u32[]{:S(2)}) collective-permute-start(bf16[14,3,16]{2,1,0:T(4,128)(2,1)S(1)} %get-tuple-element.408), channel_id=1, source_target_pairs={{4,0},{8,4},{12,8},{5,1},{9,5},{13,9},{6,2},{10,6},{14,10},{7,3},{... | collective-permute-start | bytes 4040 | tf_op jit(solution)/shard_map/ppermute | solution.py:18
  44.2 10.0 %collective-permute-start.2 = (bf16[14,3,16,128]{3,2,1,0:T(8,128)(2,1)S(1)}, bf16[14,3,16,128]{3,2,1,0:T(8,128)(2,1)S(1)}, u32[]{:S(2)}, u32[]{:S(2)}) collective-permute-start(bf16[14,3,16,128]{3,2,1,0:T(8,128)(2,1)S(1)} %get-tuple-element.401), channel_id=1, source_target_pairs={{0,4},{4,8},{8,12},{1,5},{5,9},{9,13},{2,6},{6,10},{10,14},{3,7},{... | collective-permute-start | bytes 516104 | tf_op jit(solution)/shard_map/ppermute | solution.py:15
  47.9 6.8 %collective-permute-start.3 = (bf16[14,3,16,128]{3,2,1,0:T(8,128)(2,1)S(1)}, bf16[14,3,16,128]{3,2,1,0:T(8,128)(2,1)}, u32[]{:S(2)}, u32[]{:S(2)}) collective-permute-start(bf16[14,3,16,128]{3,2,1,0:T(8,128)(2,1)S(1)} %get-tuple-element.402), channel_id=1, source_target_pairs={{4,0},{8,4},{12,8},{5,1},{9,5},{13,9},{6,2},{10,6},{14,10},{7,3},{... | collective-permute-start | bytes 516104 | tf_op jit(solution)/shard_map/ppermute | solution.py:18
  58.3 3.5 %copy-start.21 = (s32[2816]{0:T(1024)S(1)}, s32[2816]{0:T(1024)}, u32[]{:S(2)}) copy-start(s32[2816]{0:T(1024)} %fusion.26) | copy-start | bytes 33796
  61.8 4.6 %copy-start.17 = (s32[2816]{0:T(1024)}, s32[2816]{0:T(1024)S(1)}, u32[]{:S(2)}) copy-start(s32[2816]{0:T(1024)S(1)} %get-tuple-element.564) | copy-start | bytes 33796 | tf_op jit(solution)/shard_map/while
  61.8 4.6 %copy-start.19 = (s32[2816]{0:T(1024)}, s32[2816]{0:T(1024)S(1)}, u32[]{:S(2)}) copy-start(s32[2816]{0:T(1024)S(1)} %get-tuple-element.560) | copy-start | bytes 33796 | tf_op jit(solution)/shard_map/while
  61.8 4.6 %copy-start.22 = (s32[512]{0:T(512)}, s32[512]{0:T(512)S(1)}, u32[]{:S(2)}) copy-start(s32[512]{0:T(512)S(1)} %get-tuple-element.563) | copy-start | bytes 6148 | tf_op jit(solution)/shard_map/while
  61.8 4.7 %copy-start.24 = (s32[512]{0:T(512)}, s32[512]{0:T(512)S(1)}, u32[]{:S(2)}) copy-start(s32[512]{0:T(512)S(1)} %get-tuple-element.561) | copy-start | bytes 6148 | tf_op jit(solution)/shard_map/while
  65.4 6.8 %copy-start.5 = (bf16[2,16,16,1,64]{4,2,1,0,3:T(8,128)(2,1)}, bf16[2,16,16,1,64]{4,2,1,0,3:T(8,128)(2,1)S(1)}, u32[]{:S(2)}) copy-start(bf16[2,16,16,1,64]{4,2,1,0,3:T(8,128)(2,1)S(1)} %constant_dynamic-slice_fusion.7) | copy-start | bytes 196612 | tf_op jit(solution)/shard_map/while
  77.3 3.0 copy-start.1
  92.7 3.3 %copy-start.3 = (bf16[512,2816]{1,0:T(8,128)(2,1)S(1)}, bf16[512,2816]{1,0:T(8,128)(2,1)}, u32[]{:S(2)}) copy-start(bf16[512,2816]{1,0:T(8,128)(2,1)} %copy-done.2) | copy-start | bytes 8650756 | tf_op jit(solution)/shard_map/while
  98.0 4.7 %copy-start.17 = (s32[2816]{0:T(1024)}, s32[2816]{0:T(1024)S(1)}, u32[]{:S(2)}) copy-start(s32[2816]{0:T(1024)S(1)} %get-tuple-element.564) | copy-start | bytes 33796 | tf_op jit(solution)/shard_map/while
  98.0 4.7 %copy-start.19 = (s32[2816]{0:T(1024)}, s32[2816]{0:T(1024)S(1)}, u32[]{:S(2)}) copy-start(s32[2816]{0:T(1024)S(1)} %get-tuple-element.560) | copy-start | bytes 33796 | tf_op jit(solution)/shard_map/while
  98.0 4.7 %copy-start.22 = (s32[512]{0:T(512)}, s32[512]{0:T(512)S(1)}, u32[]{:S(2)}) copy-start(s32[512]{0:T(512)S(1)} %get-tuple-element.563) | copy-start | bytes 6148 | tf_op jit(solution)/shard_map/while
  98.0 4.7 %copy-start.24 = (s32[512]{0:T(512)}, s32[512]{0:T(512)S(1)}, u32[]{:S(2)}) copy-start(s32[512]{0:T(512)S(1)} %get-tuple-element.561) | copy-start | bytes 6148 | tf_op jit(solution)/shard_map/while
  101.7 6.8 %copy-start.5 = (bf16[2,16,16,1,64]{4,2,1,0,3:T(8,128)(2,1)}, bf16[2,16,16,1,64]{4,2,1,0,3:T(8,128)(2,1)S(1)}, u32[]{:S(2)}) copy-start(bf16[2,16,16,1,64]{4,2,1,0,3:T(8,128)(2,1)S(1)} %constant_dynamic-slice_fusion.7) | copy-start | bytes 196612 | tf_op jit(solution)/shard_map/while
  113.5 3.0 copy-start.1
  128.9 3.2 %copy-start.3 = (bf16[512,2816]{1,0:T(8,128)(2,1)S(1)}, bf16[512,2816]{1,0:T(8,128)(2,1)}, u32[]{:S(2)}) copy-start(bf16[512,2816]{1,0:T(8,128)(2,1)} %copy-done.2) | copy-start | bytes 8650756 | tf_op jit(solution)/shard_map/while
  134.2 4.7 %copy-start.17 = (s32[2816]{0:T(1024)}, s32[2816]{0:T(1024)S(1)}, u32[]{:S(2)}) copy-start(s32[2816]{0:T(1024)S(1)} %get-tuple-element.564) | copy-start | bytes 33796 | tf_op jit(solution)/shard_map/while
  134.2 4.7 %copy-start.19 = (s32[2816]{0:T(1024)}, s32[2816]{0:T(1024)S(1)}, u32[]{:S(2)}) copy-start(s32[2816]{0:T(1024)S(1)} %get-tuple-element.560) | copy-start | bytes 33796 | tf_op jit(solution)/shard_map/while
  134.2 4.7 %copy-start.22 = (s32[512]{0:T(512)}, s32[512]{0:T(512)S(1)}, u32[]{:S(2)}) copy-start(s32[512]{0:T(512)S(1)} %get-tuple-element.563) | copy-start | bytes 6148 | tf_op jit(solution)/shard_map/while
  134.2 4.7 %copy-start.24 = (s32[512]{0:T(512)}, s32[512]{0:T(512)S(1)}, u32[]{:S(2)}) copy-start(s32[512]{0:T(512)S(1)} %get-tuple-element.561) | copy-start | bytes 6148 | tf_op jit(solution)/shard_map/while
  137.9 6.8 %copy-start.5 = (bf16[2,16,16,1,64]{4,2,1,0,3:T(8,128)(2,1)}, bf16[2,16,16,1,64]{4,2,1,0,3:T(8,128)(2,1)S(1)}, u32[]{:S(2)}) copy-start(bf16[2,16,16,1,64]{4,2,1,0,3:T(8,128)(2,1)S(1)} %constant_dynamic-slice_fusion.7) | copy-start | bytes 196612 | tf_op jit(solution)/shard_map/while
  165.1 3.3 %copy-start.3 = (bf16[512,2816]{1,0:T(8,128)(2,1)S(1)}, bf16[512,2816]{1,0:T(8,128)(2,1)}, u32[]{:S(2)}) copy-start(bf16[512,2816]{1,0:T(8,128)(2,1)} %copy-done.2) | copy-start | bytes 8650756 | tf_op jit(solution)/shard_map/while
  170.4 4.7 %copy-start.17 = (s32[2816]{0:T(1024)}, s32[2816]{0:T(1024)S(1)}, u32[]{:S(2)}) copy-start(s32[2816]{0:T(1024)S(1)} %get-tuple-element.564) | copy-start | bytes 33796 | tf_op jit(solution)/shard_map/while
  170.4 4.7 %copy-start.19 = (s32[2816]{0:T(1024)}, s32[2816]{0:T(1024)S(1)}, u32[]{:S(2)}) copy-start(s32[2816]{0:T(1024)S(1)} %get-tuple-element.560) | copy-start | bytes 33796 | tf_op jit(solution)/shard_map/while
  170.4 4.7 %copy-start.22 = (s32[512]{0:T(512)}, s32[512]{0:T(512)S(1)}, u32[]{:S(2)}) copy-start(s32[512]{0:T(512)S(1)} %get-tuple-element.563) | copy-start | bytes 6148 | tf_op jit(solution)/shard_map/while
  170.4 4.7 %copy-start.24 = (s32[512]{0:T(512)}, s32[512]{0:T(512)S(1)}, u32[]{:S(2)}) copy-start(s32[512]{0:T(512)S(1)} %get-tuple-element.561) | copy-start | bytes 6148 | tf_op jit(solution)/shard_map/while
  174.1 6.8 %copy-start.5 = (bf16[2,16,16,1,64]{4,2,1,0,3:T(8,128)(2,1)}, bf16[2,16,16,1,64]{4,2,1,0,3:T(8,128)(2,1)S(1)}, u32[]{:S(2)}) copy-start(bf16[2,16,16,1,64]{4,2,1,0,3:T(8,128)(2,1)S(1)} %constant_dynamic-slice_fusion.7) | copy-start | bytes 196612 | tf_op jit(solution)/shard_map/while
  201.3 3.3 %copy-start.3 = (bf16[512,2816]{1,0:T(8,128)(2,1)S(1)}, bf16[512,2816]{1,0:T(8,128)(2,1)}, u32[]{:S(2)}) copy-start(bf16[512,2816]{1,0:T(8,128)(2,1)} %copy-done.2) | copy-start | bytes 8650756 | tf_op jit(solution)/shard_map/while
  206.8 8.3 %copy-start.4 = (f32[14,22,16,128]{3,2,1,0:T(8,128)S(1)}, f32[14,22,16,128]{3,2,1,0:T(8,128)}, u32[]{:S(2)}) copy-start(f32[14,22,16,128]{3,2,1,0:T(8,128)} %get-tuple-element.223) | copy-start | bytes 7569412
  208.9 9.4 %collective-permute-start.8 = (bf16[3,22,16,128]{3,2,1,0:T(8,128)(2,1)S(1)}, bf16[3,22,16,128]{3,2,1,0:T(8,128)(2,1)S(1)}, u32[]{:S(2)}, u32[]{:S(2)}) collective-permute-start(bf16[3,22,16,128]{3,2,1,0:T(8,128)(2,1)S(1)} %get-tuple-element.399), channel_id=1, source_target_pairs={{0,16},{1,17},{2,18},{3,19},{4,20},{5,21},{6,22},{7,23},{8,24},{9,... | collective-permute-start | bytes 811016 | tf_op jit(solution)/shard_map/ppermute | solution.py:15
  213.9 8.6 %collective-permute-start.9 = (bf16[3,22,16,128]{3,2,1,0:T(8,128)(2,1)S(1)}, bf16[3,22,16,128]{3,2,1,0:T(8,128)(2,1)S(1)}, u32[]{:S(2)}, u32[]{:S(2)}) collective-permute-start(bf16[3,22,16,128]{3,2,1,0:T(8,128)(2,1)S(1)} %get-tuple-element.400), channel_id=1, source_target_pairs={{16,0},{17,1},{18,2},{19,3},{20,4},{21,5},{22,6},{23,7},{24,8},{25... | collective-permute-start | bytes 811016 | tf_op jit(solution)/shard_map/ppermute | solution.py:18
  222.5 7.2 %copy-start.11 = (bf16[8,16,16,64]{3,2,1,0:T(8,128)(2,1)S(1)}, bf16[8,16,16,64]{3,2,1,0:T(8,128)(2,1)}, u32[]{:S(2)}) copy-start(bf16[8,16,16,64]{3,2,1,0:T(8,128)(2,1)} %get-tuple-element.222) | copy-start | bytes 786436
  223.4 8.3 %collective-permute-start.10 = (bf16[8,3,16,128]{3,2,1,0:T(8,128)(2,1)}, bf16[8,3,16,128]{3,2,1,0:T(8,128)(2,1)}, u32[]{:S(2)}, u32[]{:S(2)}) collective-permute-start(bf16[8,3,16,128]{3,2,1,0:T(8,128)(2,1)} %get-tuple-element.405), channel_id=1, source_target_pairs={{0,4},{4,8},{8,12},{1,5},{5,9},{9,13},{2,6},{6,10},{10,14},{3,7},{... | collective-permute-start | bytes 294920 | tf_op jit(solution)/shard_map/ppermute | solution.py:15
  227.8 6.3 %collective-permute-start.11 = (bf16[8,3,16,128]{3,2,1,0:T(8,128)(2,1)}, bf16[8,3,16,128]{3,2,1,0:T(8,128)(2,1)}, u32[]{:S(2)}, u32[]{:S(2)}) collective-permute-start(bf16[8,3,16,128]{3,2,1,0:T(8,128)(2,1)} %get-tuple-element.406), channel_id=1, source_target_pairs={{4,0},{8,4},{12,8},{5,1},{9,5},{13,9},{6,2},{10,6},{14,10},{7,3},{... | collective-permute-start | bytes 294920 | tf_op jit(solution)/shard_map/ppermute | solution.py:18
  231.7 8.9 %copy-start.13 = (bf16[2048,1,1,64]{0,3,2,1:T(8,128)(2,1)S(1)}, bf16[2048,1,1,64]{0,3,2,1:T(8,128)(2,1)}, u32[]{:S(2)}) copy-start(bf16[2048,1,1,64]{0,3,2,1:T(8,128)(2,1)} %copy.57) | copy-start | bytes 786436
  240.7 11.7 %copy-start.12 = (bf16[8,16,16,64]{3,2,1,0:T(8,128)(2,1)S(1)}, bf16[8,16,16,64]{3,2,1,0:T(8,128)(2,1)}, u32[]{:S(2)}) copy-start(bf16[8,16,16,64]{3,2,1,0:T(8,128)(2,1)} %get-tuple-element.224) | copy-start | bytes 786436
  242.0 61.7 %all-gather.2.cloned.1.call-start = ((), (), s32[]{:S(2)}) async-start(), calls=%async_computation.1 | async-start | bytes 3932160 | tf_op jit(solution)/shard_map/all_gather | solution.py:174
  (31 other events, 56.4 us)
Sparse Core Ops, SparseCore 0:
  242.1 51.3 all-reduce.1
Sparse Core Ops, SparseCore 1:
  244.0 59.6 all-gather.1
where the time goes:
time: 326 us; the launch traced here: 319 us
  local copies, waits for them, and re-layouts  89.6 us (27%)
  matrix products  58.6 us (18%)
  other arithmetic  51.7 us (16%)
  waiting for transfers between devices  37.1 us (11%)
  starting transfers between devices  35.5 us (11%)
  blocking collectives  29.8 us (9%)
  between operations  16 us (5%)
    ppermute x6, starting transfers between devices, extended(): lax.ppermute(lax.slice_in_dim(block, block.shape[dim] - width, None, axis...  25.8 us
    dot_general x4, matrix products, attend_block(): jnp.einsum('qhe,khe->hqk', query_block, keys_block, preferred_element_typ...  23.2 us
    psum x1, blocking collectives, shards(): lax.psum(part_output.astype(jnp.bfloat16), ('gx', 'gy')).astype(jnp.float32)  20.4 us
    another operation x4, local copies, waits for them, and re-layouts, attend_block(): jnp.stack([key_gradient, value_gradient], axis=2)  18.5 us
    psum x1, waiting for transfers between devices, shards(): lax.psum(part_input.astype(jnp.bfloat16), ('gx', 'gy')).astype(jnp.float32)  18.1 us
    reshape x4, local copies, waits for them, and re-layouts, attend_block(): jnp.stack([key_gradient, value_gradient], axis=2)  15.4 us
    dynamic_update_slice x4, other arithmetic, attend_block(): lax.dynamic_update_slice_in_dim(pair_sums, previous + pair_gradient, firs...  13 us
    convert_element_type x4, other arithmetic, attend_block(): (raised / jnp.sum(raised, axis=-1, keepdims=True)).astype(jnp.bfloat16)  12.1 us
  transfers between devices with their start and end apart: 14, of which 6 were waited for; matrix products, arithmetic and copies ran while one was open for 8% of the time, Pallas kernels for 0%

commit v1 on v0

v1 whole, which is shorter than its diff:
```python
import functools

import jax
import jax.numpy as jnp
import numpy as np
from jax import lax
from jax.experimental import pallas as pl
from jax.experimental.pallas import tpu as pltpu
from jax.sharding import PartitionSpec as P

HD = 64
REACH = 3
VMEM = pl.BlockSpec(memory_space=pltpu.VMEM)
SMEM = pl.BlockSpec(memory_space=pltpu.SMEM)


def dot(a, b, ca, cb):
    return lax.dot_general(a, b, (((ca,), (cb,)), ((), ())), preferred_element_type=jnp.float32)


def shift(array, axis, up):
    count = lax.axis_size(axis)
    pairs = [(i, i + 1) for i in range(count - 1)]
    if not up:
        pairs = [(b, a) for a, b in pairs]
    return lax.ppermute(array, axis, pairs)


def tile_of(extent):
    return 4 if extent % 4 == 0 else extent


def mask_table(bx, by, depth):
    kx, ky = bx + 2 * REACH, by + 2 * REACH
    kg = np.stack(np.meshgrid(np.arange(kx) - REACH, np.arange(ky) - REACH, np.arange(depth), indexing="ij"), -1)
    qg = np.stack(np.meshgrid(np.arange(bx), np.arange(by), np.arange(depth), indexing="ij"), -1)
    far = np.abs(kg.reshape(-1, 1, 3) - qg.reshape(1, -1, 3)).max(-1)
    return ((far <= REACH).astype(np.float32) + (far == 0)).astype(np.float32)


def attend_kernel(
    depth, bx, by, tok, cot, wq, wo, kv, xlo, xhi, ylo, yhi, bits, table, dq_ref, acc, wg, kvp, gate
):
    nx, ny = tok.shape[0], tok.shape[1] // depth
    rim = REACH * depth
    rows = ny * depth
    scale = HD ** (-0.5)
    kvp[REACH : REACH + nx, rim : rim + rows] = kv[...]
    kvp[:REACH, rim : rim + rows] = xlo[...]
    kvp[REACH + nx :, rim : rim + rows] = xhi[...]
    kvp[:, :rim] = ylo[...]
    kvp[:, rim + rows :] = yhi[...]
    acc[...] = jnp.zeros_like(acc)
    wg[...] = jnp.zeros_like(wg)
    z = lax.broadcasted_iota(jnp.int32, (depth, 128), 0)

    def fill(x, carry):
        for y in range(ny + 2 * REACH):
            live = jnp.right_shift(jnp.full((depth, 128), bits[x, y], jnp.int32), z) & 1
            gate[x, y * depth : (y + 1) * depth, :] = 1.0 - live.astype(jnp.float32)
        return carry

    lax.fori_loop(0, nx + 2 * REACH, fill, 0)
    kx, kr = bx + 2 * REACH, (by + 2 * REACH) * depth
    qr = by * depth
    nq, nk = bx * qr, kx * kr
    across = ny // by

    def body(i, carry):
        x0 = (i // across) * bx
        r0 = pl.multiple_of((i % across) * qr, qr)
        mine = (pl.ds(x0, bx), pl.ds(r0, qr))
        wide = (pl.ds(x0, kx), pl.ds(r0, kr))
        tb = tok[mine].reshape(nq, -1)
        cb = cot[mine].reshape(nq, -1)
        q = (dot(tb, wq[...], 1, 0).astype(jnp.bfloat16).astype(jnp.float32) * scale).astype(jnp.bfloat16)
        u = dot(cb, wo[...], 1, 1).astype(jnp.bfloat16)
        keys = kvp[wide].reshape(nk, 2 * HD)
        g1 = gate[wide].reshape(nk, 128)
        g1 = jnp.concatenate([g1] * (nq // 128), axis=1)
        s = jnp.where(table[...] > g1, dot(keys, q, 1, 1), -1e30)
        e = jnp.exp(s - jnp.max(s, axis=0, keepdims=True))
        p = (e * (1.0 / jnp.sum(e, axis=0, keepdims=True))).astype(jnp.bfloat16)
        o = dot(keys, p, 0, 0)
        r = jnp.sum(u.astype(jnp.float32).T * o, axis=0, keepdims=True)
        g = dot(keys, u, 1, 1)
        ds = (p.astype(jnp.float32) * (g - r)).astype(jnp.bfloat16)
        dq = dot(keys, ds, 0, 0) * scale
        dkv = dot(ds, q, 1, 0) + dot(p, u, 1, 0)
        acc[wide] += dkv.reshape(kx, kr, 2 * HD)
        wg[:HD] += dot(dq[:HD].astype(jnp.bfloat16), tb, 1, 0)
        wg[HD:] += dot(o[HD:].astype(jnp.bfloat16), cb, 1, 0)
        dq_ref[mine] = dq.T.astype(jnp.bfloat16).reshape(bx, qr, 2 * HD)
        return carry

    lax.fori_loop(0, (nx // bx) * across, body, 0)


def tail_kernel(rim, tok, dq, acc, xlo, xhi, ylo, yhi, wq, wkv, wg, part, grads, cen):
    nx, rows = tok.shape[0], tok.shape[1]
    cen[...] = acc[REACH : REACH + nx, rim : rim + rows]
    cen[:REACH] += xlo[:, rim : rim + rows].astype(jnp.float32)
    cen[nx - REACH :] += xhi[:, rim : rim + rows].astype(jnp.float32)
    cen[:, :rim] += ylo[...].astype(jnp.float32)
    cen[:, rows - rim :] += yhi[...].astype(jnp.float32)
    total = jnp.zeros((2 * HD, tok.shape[2]), jnp.float32)
    for x in range(nx):
        dkv = cen[x].astype(jnp.bfloat16)
        part[x] = (dot(dkv, wkv[...], 1, 1) + dot(dq[x], wq[...], 1, 1)).astype(jnp.bfloat16)
        total += dot(dkv, tok[x], 0, 0)
    grads[: 2 * HD] = wg[...].astype(jnp.bfloat16)
    grads[2 * HD :] = total.astype(jnp.bfloat16)


def window_bits(tissue_bits):
    nx, ny = tissue_bits.shape
    whole = lax.all_gather(tissue_bits, ("gx", "gy"))
    cx, cy = lax.axis_size("gx"), lax.axis_size("gy")
    whole = whole.reshape(cx, cy, nx, ny).transpose(0, 2, 1, 3).reshape(cx * nx, cy * ny)
    whole = jnp.pad(whole, REACH)
    start = (lax.axis_index("gx") * nx, lax.axis_index("gy") * ny)
    return lax.dynamic_slice(whole, start, (nx + 2 * REACH, ny + 2 * REACH))


def shards(tokens, input_weight, output_weight, tissue_bits, cotangent):
    nx, ny, depth, width = tokens.shape
    rows, rim = ny * depth, REACH * depth
    tok = tokens.reshape(nx, rows, width)
    cot = cotangent.reshape(nx, rows, width)
    wq = jnp.pad(input_weight[:, :HD], ((0, 0), (0, HD)))
    wkv = input_weight[:, HD:]
    wo = jnp.pad(output_weight, ((HD, 0), (0, 0)))
    bits = window_bits(tissue_bits)
    kv = (
        jnp.dot(tok.reshape(nx * rows, width), wkv, preferred_element_type=jnp.float32)
        .astype(jnp.bfloat16)
        .reshape(nx, rows, 2 * HD)
    )
    xlo = shift(kv[nx - REACH :], "gx", True)
    xhi = shift(kv[:REACH], "gx", False)
    top = jnp.concatenate([xlo[:, rows - rim :], kv[:, rows - rim :], xhi[:, rows - rim :]], axis=0)
    bottom = jnp.concatenate([xlo[:, :rim], kv[:, :rim], xhi[:, :rim]], axis=0)
    ylo = shift(top, "gy", True)
    yhi = shift(bottom, "gy", False)
    bx, by = tile_of(nx), tile_of(ny)
    table = jnp.asarray(mask_table(bx, by, depth))
    px, pr = nx + 2 * REACH, rows + 2 * rim
    dq, acc, wg = pl.pallas_call(
        functools.partial(attend_kernel, depth, bx, by),
        out_shape=(
            jax.ShapeDtypeStruct((nx, rows, 2 * HD), jnp.bfloat16),
            jax.ShapeDtypeStruct((px, pr, 2 * HD), jnp.float32),
            jax.ShapeDtypeStruct((2 * HD, width), jnp.float32),
        ),
        in_specs=[VMEM] * 9 + [SMEM, VMEM],
        out_specs=(VMEM,) * 3,
        scratch_shapes=[
            pltpu.VMEM((px, pr, 2 * HD), jnp.bfloat16),
            pltpu.VMEM((px, pr, 128), jnp.float32),
        ],
        compiler_params=pltpu.CompilerParams(vmem_limit_bytes=48 * 1024 * 1024),
        name="attend",
    )(tok, cot, wq, wo, kv, xlo, xhi, ylo, yhi, bits, table)

    dxlo = shift(acc[REACH + nx :].astype(jnp.bfloat16), "gx", True)
    dxhi = shift(acc[:REACH].astype(jnp.bfloat16), "gx", False)

    def edge(lo, hi):
        mine = acc[REACH : REACH + nx, lo:hi]
        below = jnp.pad(dxlo[:, lo:hi].astype(jnp.float32), ((0, nx - REACH), (0, 0), (0, 0)))
        above = jnp.pad(dxhi[:, lo:hi].astype(jnp.float32), ((nx - REACH, 0), (0, 0), (0, 0)))
        return (mine + below + above).astype(jnp.bfloat16)

    dylo = shift(edge(rim + rows, pr), "gy", True)
    dyhi = shift(edge(0, rim), "gy", False)
    part, grads = pl.pallas_call(
        functools.partial(tail_kernel, rim),
        out_shape=(
            jax.ShapeDtypeStruct((nx, rows, width), jnp.bfloat16),
            jax.ShapeDtypeStruct((4 * HD, width), jnp.bfloat16),
        ),
        in_specs=[VMEM] * 10,
        out_specs=(VMEM,) * 2,
        scratch_shapes=[pltpu.VMEM((nx, rows, 2 * HD), jnp.float32)],
        compiler_params=pltpu.CompilerParams(vmem_limit_bytes=48 * 1024 * 1024),
        name="tail",
    )(tok, dq, acc, dxlo, dxhi, dylo, dyhi, wq, wkv, wg)
    token_gradient = lax.psum_scatter(
        part.reshape(nx * rows, width), "ha", scatter_dimension=1, tiled=True
    ).reshape(nx, ny, depth, -1)
    count = nx * rows * lax.axis_size("gx") * lax.axis_size("gy")
    summed = lax.psum(grads, ("gx", "gy")).astype(jnp.float32) * count ** (-0.5)
    turned = jnp.concatenate([summed[:HD], summed[2 * HD :]], axis=0).T
    return token_gradient, turned, summed[HD : 2 * HD]


def solution(mesh):
    placed = (
        P("gx", "gy", None, None),
        P(None, "ha"),
        P("ha", None),
        P("gx", "gy"),
        P("gx", "gy", None, None),
    )
    return jax.shard_map(
        shards,
        mesh=mesh,
        in_specs=placed,
        out_specs=(P("gx", "gy", None, "ha"), P(None, "ha"), P("ha", None)),
        check_vma=False,
    )
```

time: 326 us -> 160 us (0.49); the launches traced: 319 us -> 157 us
  local copies, waits for them, and re-layouts: 89.6 us -> 13.1 us
  matrix products: 58.6 us -> 2.01 us
  other arithmetic: 51.7 us -> 5.05 us
  Pallas kernels: 0 us -> 27.6 us
  waiting for transfers between devices: 37.1 us -> 62.1 us
  blocking collectives: 29.8 us -> 11 us
  starting transfers between devices: 35.5 us -> 20.8 us
    dot_general x29 -> x1, matrix products: 58.6 us -> 2.01 us  [shards(): jnp.dot(tok.reshape(nx * rows, width), wkv, preferred_element_type=jnp.fl...]
    psum x1, waiting for transfers between devices: 18.1 us -> 53.5 us  [shards(): summed = lax.psum(grads, ('gx', 'gy')).astype(jnp.float32) * count ** (-0.5)]
    pallas_call x0 -> x2, Pallas kernels: none -> 27.6 us  [the longest x1 24.6 us: shards(): pl.pallas_call(functools.partial(attend_kernel, depth, bx, by), out_shape...]
    reshape x9 -> x2, local copies, waits for them, and re-layouts: 22.2 us -> 0.09 us  [window_bits(): whole.reshape(cx, cy, nx, ny).transpose(0, 2, 1, 3)]
    psum x1 -> x0, blocking collectives: 20.4 us -> none  [shards(): lax.psum(part_output.astype(jnp.bfloat16), ('gx', 'gy')).astype(jnp.float32)]
    another operation x4 -> x0, local copies, waits for them, and re-layouts: 18.5 us -> none  [attend_block(): jnp.stack([key_gradient, value_gradient], axis=2)]
    dynamic_slice x16 -> x1, local copies, waits for them, and re-layouts: 18 us -> 0.1 us  [window_bits(): return lax.dynamic_slice(whole, start, (nx + 2 * REACH, ny + 2 * REACH))]
    ppermute x12 -> x8, starting transfers between devices: 35.4 us -> 20.7 us  [shift(): return lax.ppermute(array, axis, pairs)]
  transfers between devices with their start and end apart: 14 -> 10, of which waited for: 6 -> 6; matrix products, arithmetic and copies ran while one was open for 8% -> 3% of each run, Pallas kernels for 0% -> 0%
where the time goes in v1:
time: 160 us; the launch traced here: 157 us
  waiting for transfers between devices  62.1 us (39%)
  Pallas kernels  27.6 us (17%)
  starting transfers between devices  20.8 us (13%)
  between operations  15.8 us (10%)
  local copies, waits for them, and re-layouts  13.1 us (8%)
  blocking collectives  11 us (7%)
  other arithmetic  5.05 us (3%)
  matrix products  2.01 us (1%)
    psum x1, waiting for transfers between devices, shards(): summed = lax.psum(grads, ('gx', 'gy')).astype(jnp.float32) * count ** (-0.5)  53.5 us
    pallas_call x1, Pallas kernels, shards(): pl.pallas_call(functools.partial(attend_kernel, depth, bx, by), out_shape...  24.6 us
    ppermute x8, starting transfers between devices, shift(): return lax.ppermute(array, axis, pairs)  20.7 us
    unnamed x41, local copies, waits for them, and re-layouts  12.1 us
    all_gather x1, blocking collectives, window_bits(): whole = lax.all_gather(tissue_bits, ('gx', 'gy'))  11 us
    ppermute x8, waiting for transfers between devices, shift(): return lax.ppermute(array, axis, pairs)  8.57 us
  transfers between devices with their start and end apart: 10, of which 6 were waited for; matrix products, arithmetic and copies ran while one was open for 3% of the time, Pallas kernels for 0%

profile of v1, /device:TPU:9, one launch (start us, length us, event | category | flops | bytes accessed | tf_op | source)
XLA Modules:
  0.0 157.4 jit_solution(18405005005408870654)
XLA Ops:
  8.0 0.0 all-reduce.8.cloned.1.call-start
  8.1 2.0 %convolution_convert_fusion = bf16[2048,128]{1,0:T(8,128)(2,1)S(1)} fusion(bf16[2048,384]{1,0:T(8,128)(2,1)} %bitcast.17, bf16[384,192]{0,1:T(8,128)(2,1)} %param.7), kind=kOutput, calls=%fused_computation | convolution fusion | flops 201588736 | bytes 2195456 | tf_op jit(solution)/shard_map/dot_general | solution.py:135
  10.1 0.0 copy-start.17
  10.1 0.0 copy-start
  10.2 3.3 %collective-permute-start = (bf16[3,256,128]{2,1,0:T(8,128)(2,1)S(1)}, bf16[3,256,128]{2,1,0:T(8,128)(2,1)S(1)}, u32[]{:S(2)}, u32[]{:S(2)}) collective-permute-start(bf16[3,256,128]{2,1,0:T(8,128)(2,1)S(1)} %bitcast.28), channel_id=1, source_target_pairs={{0,16},{1,17},{2,18},{3,19},{4,20},{5,21},{6,22},{7,23},{8,24},{9,... | collective-permute-start | bytes 589832 | tf_op jit(solution)/shard_map/ppermute | solution.py:26
  13.4 1.3 collective-permute-start.1
  14.8 11.0 %all-gather = s32[64,16]{1,0:T(8,128)S(1)} all-gather(s32[8,16]{1,0:T(8,128)S(1)} %copy-done.16), channel_id=2, replica_groups=mesh['gx'=2,'gy'=4,'ha'=4] {'gx','gy'}, dimensions={0}, use_global_device_ids=true | all-gather | bytes 4608 | tf_op jit(solution)/shard_map/all_gather | solution.py:117
  25.8 0.1 reshape.33
  25.8 0.1 copy.17
  26.0 0.0 copy-start.1
  26.0 0.1 pad_dynamic-slice_fusion.bits
  26.1 0.0 collective-permute-done.xlo
  26.2 3.4 %collective-permute-start.2 = (bf16[14,48,128]{2,1,0:T(8,128)(2,1)S(1)}, bf16[14,48,128]{2,1,0:T(8,128)(2,1)S(1)}, u32[]{:S(2)}, u32[]{:S(2)}) collective-permute-start(bf16[14,48,128]{2,1,0:T(8,128)(2,1)S(1)} %pad_maximum_fusion), channel_id=1, source_target_pairs={{0,4},{4,8},{8,12},{1,5},{5,9},{9,13},{2,6},{6,10},{10,14},{3,7},{... | collective-permute-start | bytes 516104 | tf_op jit(solution)/shard_map/ppermute | solution.py:26
  29.6 1.9 %collective-permute-start.3 = (bf16[14,48,128]{2,1,0:T(8,128)(2,1)S(1)}, bf16[14,48,128]{2,1,0:T(8,128)(2,1)S(1)}, u32[]{:S(2)}, u32[]{:S(2)}) collective-permute-start(bf16[14,48,128]{2,1,0:T(8,128)(2,1)S(1)} %pad_maximum_fusion.1), channel_id=1, source_target_pairs={{4,0},{8,4},{12,8},{5,1},{9,5},{13,9},{6,2},{10,6},{14,10},{7,3},{... | collective-permute-start | bytes 516104 | tf_op jit(solution)/shard_map/ppermute | solution.py:26
  31.6 0.3 collective-permute-done.2.ylo
  31.9 4.4 %collective-permute-done.3.yhi = bf16[14,48,128]{2,1,0:T(8,128)(2,1)S(1)} collective-permute-done((bf16[14,48,128]{2,1,0:T(8,128)(2,1)S(1)}, bf16[14,48,128]{2,1,0:T(8,128)(2,1)S(1)}, u32[]{:S(2)}, u32[]{:S(2)}) %collective-permute-start.3) | collective-permute-done | bytes 172064 | tf_op jit(solution)/shard_map/ppermute | solution.py:26
  36.3 24.6 %attend.1 = (bf16[8,256,128]{2,1,0:T(8,128)(2,1)S(1)}, f32[14,352,128]{2,1,0:T(8,128)}, f32[128,384]{1,0:T(8,128)S(1)}) custom-call(bf16[8,256,384]{2,1,0:T(8,128)(2,1)S(1)} %bitcast.18, bf16[8,256,384]{2,1,0:T(8,128)(2,1)S(1)} %bitcast.23, bf16[384,128]{1,0:T(8,128)(2,1)S(1)} %broadcast_select_fusion.wq, bf16[128,384]{1,0:T(8,128)(2,1)S(1)} %pad.39.wo, ...), custom_call_target="tpu_custom_call" | custom-call | tf_op jit(solution)/shard_map/attend/pallas_call | solution.py:148
  61.0 2.1 %convert.12 = bf16[14,352,128]{2,1,0:T(8,128)(2,1)S(1)} convert(f32[14,352,128]{2,1,0:T(8,128)} %get-tuple-element.9.acc) | non-fusion elementwise | flops 630784 | bytes 3784704 | tf_op jit(solution)/shard_map/convert.9
  63.2 1.3 collective-permute-start.5
  64.5 4.0 %collective-permute-start.4 = (bf16[3,352,128]{2,1,0:T(8,128)(2,1)S(1)}, bf16[3,352,128]{2,1,0:T(8,128)(2,1)S(1)}, u32[]{:S(2)}, u32[]{:S(2)}) collective-permute-start(bf16[3,352,128]{2,1,0:T(8,128)(2,1)S(1)} %get-tuple-element.16), channel_id=1, source_target_pairs={{0,16},{1,17},{2,18},{3,19},{4,20},{5,21},{6,22},{7,23},{8,24},{9,... | collective-permute-start | bytes 811016 | tf_op jit(solution)/shard_map/ppermute | solution.py:26
  68.5 1.9 %collective-permute-done.5.xhi = bf16[3,352,128]{2,1,0:T(8,128)(2,1)S(1)} collective-permute-done((bf16[3,352,128]{2,1,0:T(8,128)(2,1)S(1)}, bf16[3,352,128]{2,1,0:T(8,128)(2,1)S(1)}, u32[]{:S(2)}, u32[]{:S(2)}) %collective-permute-start.5) | collective-permute-done | bytes 270368 | tf_op jit(solution)/shard_map/ppermute | solution.py:26
  70.4 1.7 %collective-permute-done.4.xlo = bf16[3,352,128]{2,1,0:T(8,128)(2,1)S(1)} collective-permute-done((bf16[3,352,128]{2,1,0:T(8,128)(2,1)S(1)}, bf16[3,352,128]{2,1,0:T(8,128)(2,1)S(1)}, u32[]{:S(2)}, u32[]{:S(2)}) %collective-permute-start.4) | collective-permute-done | bytes 270368 | tf_op jit(solution)/shard_map/ppermute | solution.py:26
  72.1 1.2 add_convert_fusion
  73.3 1.9 %collective-permute-start.7 = (bf16[8,48,128]{2,1,0:T(8,128)(2,1)S(1)}, bf16[8,48,128]{2,1,0:T(8,128)(2,1)S(1)}, u32[]{:S(2)}, u32[]{:S(2)}) collective-permute-start(bf16[8,48,128]{2,1,0:T(8,128)(2,1)S(1)} %get-tuple-element.13), channel_id=1, source_target_pairs={{4,0},{8,4},{12,8},{5,1},{9,5},{13,9},{6,2},{10,6},{14,10},{7,3},{... | collective-permute-start | bytes 294920 | tf_op jit(solution)/shard_map/ppermute | solution.py:26
  75.2 3.6 %collective-permute-start.6 = (bf16[8,48,128]{2,1,0:T(8,128)(2,1)S(1)}, bf16[8,48,128]{2,1,0:T(8,128)(2,1)S(1)}, u32[]{:S(2)}, u32[]{:S(2)}) collective-permute-start(bf16[8,48,128]{2,1,0:T(8,128)(2,1)S(1)} %get-tuple-element.14), channel_id=1, source_target_pairs={{0,4},{4,8},{8,12},{1,5},{5,9},{9,13},{2,6},{6,10},{10,14},{3,7},{... | collective-permute-start | bytes 294920 | tf_op jit(solution)/shard_map/ppermute | solution.py:26
  78.8 0.8 copy.18.wkv
  79.6 0.0 collective-permute-done.7.yhi
  79.6 0.6 copy-done.10
  80.3 0.2 collective-permute-done.6.ylo
  80.5 0.6 copy-done.12
  81.1 1.0 copy-done.3
  82.2 1.0 copy-done.5
  83.1 0.9 copy-done.6
  84.0 0.9 copy-done.8
  84.9 0.9 copy-done.11
  85.8 0.9 copy-done.13
  86.7 3.0 %tail.1 = (bf16[8,256,384]{2,1,0:T(8,128)(2,1)S(1)}, bf16[256,384]{1,0:T(8,128)(2,1)S(1)}) custom-call(bf16[8,256,384]{2,1,0:T(8,128)(2,1)S(1)} %bitcast.19, bf16[8,256,128]{2,1,0:T(8,128)(2,1)S(1)} %copy-done.3, f32[14,352,128]{2,1,0:T(8,128)} %get-tuple-element.9.acc, bf16[3,352,128]{2,1,0:T(8,128)(2,1)S(1)} %copy-done.5, ...), custom_call_target="tpu_custom_call" | custom-call | tf_op jit(solution)/shard_map/tail/pallas_call | solution.py:176
  89.7 0.0 copy-start.9
  89.7 0.7 copy-done.9
  90.4 0.0 all-reduce.8.cloned.1.call-update
  90.4 0.0 reduce-scatter.4.cloned.1.call-start
  90.5 1.6 %copy.15 = bf16[2048,384]{0,1:T(8,128)(2,1)} copy(bf16[2048,384]{1,0:T(8,128)(2,1)S(1)} %bitcast.22) | data formatting | bytes 3145728
  92.1 0.0 reduce-scatter.4.cloned.1.call-update
  92.1 53.5 %all-reduce.8.cloned.1.call-done = bf16[256,384]{1,0:T(8,128)(2,1)} async-done(((bf16[256,384]{1,0:T(8,128)(2,1)}), bf16[256,384]{1,0:T(8,128)(2,1)}) %all-reduce.8.cloned.1.call-update) | async-done | bytes 196624 | tf_op jit(solution)/shard_map/psum | solution.py:192
  145.6 1.0 convert_multiply_fusion
  146.6 0.7 fusion.4
  147.3 0.7 maximum_bitcast_fusion
  148.0 2.0 %copy.16 = bf16[2048,96]{1,0:T(8,128)(2,1)} copy(bf16[2048,96]{0,1:T(8,128)(2,1)} %bitcast.26) | data formatting | bytes 786432
  (39 shorter events, 0.3 us)
Async XLA Ops:
  8.0 6.7 %copy-start.14 = (bf16[384,192]{0,1:T(8,128)(2,1)S(1)}, bf16[384,192]{0,1:T(8,128)(2,1)}, u32[]{:S(2)}) copy-start(bf16[384,192]{0,1:T(8,128)(2,1)} %param.7) | copy-start | bytes 442372
  8.0 137.6 %all-reduce.8.cloned.1.call-start = ((), (), s32[]{:S(2)}) async-start(), calls=%async_computation.1 | async-start | bytes 393216 | tf_op jit(solution)/shard_map/psum | solution.py:192
  8.1 6.7 %copy-start.16 = (s32[8,16]{1,0:T(8,128)S(1)}, s32[8,16]{1,0:T(8,128)}, u32[]{:S(2)}) copy-start(s32[8,16]{1,0:T(8,128)} %param.9) | copy-start | bytes 1540
  8.1 17.9 %copy-start.15 = (bf16[64,384]{1,0:T(8,128)(2,1)S(1)}, bf16[64,384]{1,0:T(8,128)(2,1)}, u32[]{:S(2)}) copy-start(bf16[64,384]{1,0:T(8,128)(2,1)} %param.8) | copy-start | bytes 147460
  10.1 21.4 %copy-start.17 = (pred[128]{0:T(512)(128)(4,1)S(1)}, pred[128]{0:T(512)(128)(4,1)}, u32[]{:S(2)}) copy-start(pred[128]{0:T(512)(128)(4,1)} %constant.9.clone.1) | copy-start | bytes 388
  10.1 26.2 %copy-start = (bf16[8,16,16,384]{3,2,1,0:T(8,128)(2,1)S(1)}, bf16[8,16,16,384]{3,2,1,0:T(8,128)(2,1)}, u32[]{:S(2)}) copy-start(bf16[8,16,16,384]{3,2,1,0:T(8,128)(2,1)} %param.6) | copy-start | bytes 4718596
  10.2 16.0 %collective-permute-start = (bf16[3,256,128]{2,1,0:T(8,128)(2,1)S(1)}, bf16[3,256,128]{2,1,0:T(8,128)(2,1)S(1)}, u32[]{:S(2)}, u32[]{:S(2)}) collective-permute-start(bf16[3,256,128]{2,1,0:T(8,128)(2,1)S(1)} %bitcast.28), channel_id=1, source_target_pairs={{0,16},{1,17},{2,18},{3,19},{4,20},{5,21},{6,22},{7,23},{8,24},{9,... | collective-permute-start | bytes 589832 | tf_op jit(solution)/shard_map/ppermute | solution.py:26
  13.4 12.7 %collective-permute-start.1 = (bf16[3,256,128]{2,1,0:T(8,128)(2,1)S(1)}, bf16[3,256,128]{2,1,0:T(8,128)(2,1)S(1)}, u32[]{:S(2)}, u32[]{:S(2)}) collective-permute-start(bf16[3,256,128]{2,1,0:T(8,128)(2,1)S(1)} %bitcast.27), channel_id=1, source_target_pairs={{16,0},{17,1},{18,2},{19,3},{20,4},{21,5},{22,6},{23,7},{24,8},{25... | collective-permute-start | bytes 589832 | tf_op jit(solution)/shard_map/ppermute | solution.py:26
  26.0 10.4 %copy-start.1 = (bf16[8,16,16,384]{3,2,1,0:T(8,128)(2,1)S(1)}, bf16[8,16,16,384]{3,2,1,0:T(8,128)(2,1)}, u32[]{:S(2)}) copy-start(bf16[8,16,16,384]{3,2,1,0:T(8,128)(2,1)} %param.10) | copy-start | bytes 4718596
  26.2 5.7 %collective-permute-start.2 = (bf16[14,48,128]{2,1,0:T(8,128)(2,1)S(1)}, bf16[14,48,128]{2,1,0:T(8,128)(2,1)S(1)}, u32[]{:S(2)}, u32[]{:S(2)}) collective-permute-start(bf16[14,48,128]{2,1,0:T(8,128)(2,1)S(1)} %pad_maximum_fusion), channel_id=1, source_target_pairs={{0,4},{4,8},{8,12},{1,5},{5,9},{9,13},{2,6},{6,10},{10,14},{3,7},{... | collective-permute-start | bytes 516104 | tf_op jit(solution)/shard_map/ppermute | solution.py:26
  29.6 6.7 %collective-permute-start.3 = (bf16[14,48,128]{2,1,0:T(8,128)(2,1)S(1)}, bf16[14,48,128]{2,1,0:T(8,128)(2,1)S(1)}, u32[]{:S(2)}, u32[]{:S(2)}) collective-permute-start(bf16[14,48,128]{2,1,0:T(8,128)(2,1)S(1)} %pad_maximum_fusion.1), channel_id=1, source_target_pairs={{4,0},{8,4},{12,8},{5,1},{9,5},{13,9},{6,2},{10,6},{14,10},{7,3},{... | collective-permute-start | bytes 516104 | tf_op jit(solution)/shard_map/ppermute | solution.py:26
  61.0 2.1 %copy-start.2 = (bf16[8,256,128]{2,1,0:T(8,128)(2,1)}, bf16[8,256,128]{2,1,0:T(8,128)(2,1)S(1)}, u32[]{:S(2)}) copy-start(bf16[8,256,128]{2,1,0:T(8,128)(2,1)S(1)} %get-tuple-element.8.dq) | copy-start | bytes 1572868
  61.0 2.2 %copy-start.7 = (f32[128,384]{1,0:T(8,128)}, f32[128,384]{1,0:T(8,128)S(1)}, u32[]{:S(2)}) copy-start(f32[128,384]{1,0:T(8,128)S(1)} %get-tuple-element.10.wg) | copy-start | bytes 589828
  63.2 7.2 %collective-permute-start.5 = (bf16[3,352,128]{2,1,0:T(8,128)(2,1)S(1)}, bf16[3,352,128]{2,1,0:T(8,128)(2,1)S(1)}, u32[]{:S(2)}, u32[]{:S(2)}) collective-permute-start(bf16[3,352,128]{2,1,0:T(8,128)(2,1)S(1)} %get-tuple-element.15), channel_id=1, source_target_pairs={{16,0},{17,1},{18,2},{19,3},{20,4},{21,5},{22,6},{23,7},{24,8},{25... | collective-permute-start | bytes 811016 | tf_op jit(solution)/shard_map/ppermute | solution.py:26
  64.5 7.6 %collective-permute-start.4 = (bf16[3,352,128]{2,1,0:T(8,128)(2,1)S(1)}, bf16[3,352,128]{2,1,0:T(8,128)(2,1)S(1)}, u32[]{:S(2)}, u32[]{:S(2)}) collective-permute-start(bf16[3,352,128]{2,1,0:T(8,128)(2,1)S(1)} %get-tuple-element.16), channel_id=1, source_target_pairs={{0,16},{1,17},{2,18},{3,19},{4,20},{5,21},{6,22},{7,23},{8,24},{9,... | collective-permute-start | bytes 811016 | tf_op jit(solution)/shard_map/ppermute | solution.py:26
  72.1 9.0 %copy-start.4 = (bf16[3,352,128]{2,1,0:T(8,128)(2,1)}, bf16[3,352,128]{2,1,0:T(8,128)(2,1)S(1)}, u32[]{:S(2)}) copy-start(bf16[3,352,128]{2,1,0:T(8,128)(2,1)S(1)} %collective-permute-done.4.xlo) | copy-start | bytes 811012
  73.3 6.4 %collective-permute-start.7 = (bf16[8,48,128]{2,1,0:T(8,128)(2,1)S(1)}, bf16[8,48,128]{2,1,0:T(8,128)(2,1)S(1)}, u32[]{:S(2)}, u32[]{:S(2)}) collective-permute-start(bf16[8,48,128]{2,1,0:T(8,128)(2,1)S(1)} %get-tuple-element.13), channel_id=1, source_target_pairs={{4,0},{8,4},{12,8},{5,1},{9,5},{13,9},{6,2},{10,6},{14,10},{7,3},{... | collective-permute-start | bytes 294920 | tf_op jit(solution)/shard_map/ppermute | solution.py:26
  75.2 5.3 %collective-permute-start.6 = (bf16[8,48,128]{2,1,0:T(8,128)(2,1)S(1)}, bf16[8,48,128]{2,1,0:T(8,128)(2,1)S(1)}, u32[]{:S(2)}, u32[]{:S(2)}) collective-permute-start(bf16[8,48,128]{2,1,0:T(8,128)(2,1)S(1)} %get-tuple-element.14), channel_id=1, source_target_pairs={{0,4},{4,8},{8,12},{1,5},{5,9},{9,13},{2,6},{6,10},{10,14},{3,7},{... | collective-permute-start | bytes 294920 | tf_op jit(solution)/shard_map/ppermute | solution.py:26
  79.6 0.6 copy-start.10
  80.5 0.6 copy-start.12
  81.1 1.0 copy-start.3
  82.2 1.0 copy-start.5
  83.1 0.9 copy-start.6
  84.0 0.9 copy-start.8
  84.9 0.9 copy-start.11
  85.8 0.9 copy-start.13
  89.7 0.7 copy-start.9
  90.4 57.6 %reduce-scatter.4.cloned.1.call-start = ((), (), s32[]{:S(2)}) async-start(), calls=%async_computation.2 | async-start | bytes 1966080
Sparse Core Ops, SparseCore 0:
  90.5 55.0 all-reduce.7
Sparse Core Ops, SparseCore 1:
  93.2 35.6 reduce-scatter.3

commit v2 on v1

v2 whole, which is shorter than its diff:
```python
import functools

import jax
import jax.numpy as jnp
import numpy as np
from jax import lax
from jax.experimental import pallas as pl
from jax.experimental.pallas import tpu as pltpu
from jax.sharding import PartitionSpec as P

HD = 64
REACH = 3
VMEM = pl.BlockSpec(memory_space=pltpu.VMEM)
SMEM = pl.BlockSpec(memory_space=pltpu.SMEM)
MESH = pl.DeviceIdType.MESH


def dot(a, b, ca, cb):
    return lax.dot_general(a, b, (((ca,), (cb,)), ((), ())), preferred_element_type=jnp.float32)


def tile_of(extent):
    return 4 if extent % 4 == 0 else extent


def mask_table(bx, by, depth):
    kx, ky = bx + 2 * REACH, by + 2 * REACH
    kg = np.stack(np.meshgrid(np.arange(kx) - REACH, np.arange(ky) - REACH, np.arange(depth), indexing="ij"), -1)
    qg = np.stack(np.meshgrid(np.arange(bx), np.arange(by), np.arange(depth), indexing="ij"), -1)
    far = np.abs(kg.reshape(-1, 1, 3) - qg.reshape(1, -1, 3)).max(-1)
    return ((far <= REACH).astype(np.float32) + (far == 0)).astype(np.float32)


def send(src, dst, send_sem, recv_sem, where):
    return pltpu.make_async_remote_copy(
        src_ref=src, dst_ref=dst, send_sem=send_sem, recv_sem=recv_sem, device_id=where, device_id_type=MESH
    )


def swap(axis, count, to_low, to_high):
    me = lax.axis_index(axis)
    has_low, has_high = me > 0, me < count - 1

    @pl.when(has_low)
    def _():
        to_low.start()

    @pl.when(has_high)
    def _():
        to_high.start()

    @pl.when(has_low)
    def _():
        to_low.wait_send()
        to_high.wait_recv()

    @pl.when(has_high)
    def _():
        to_high.wait_send()
        to_low.wait_recv()


def kernel(
    sizes, depth, bx, by, tok, cot, wq, wkv, wo, bits, table,
    token_out, input_out, output_out,
    kvg, acc, wg, dq_all, cen, dkv_all, sx, rx, sy, ry, psend, precv, own, gsrc, grecv, gsum,
    sem_h, sem_hr, sem_p, sem_pr, sem_g, sem_gr, sem_b, sem_br,
):
    cx, cy, ch = sizes
    nx, rows = tok.shape[0], tok.shape[1]
    ny, width = rows // depth, tok.shape[2]
    rim = REACH * depth
    scale = HD ** (-0.5)
    ix, iy, ih = lax.axis_index("gx"), lax.axis_index("gy"), lax.axis_index("ha")
    n = cx * cy
    flat = ix * cy + iy

    def peer(k):
        t = lax.rem(flat + k, n)
        return t, {"gx": t // cy, "gy": lax.rem(t, cy)}

    barrier = pltpu.get_barrier_semaphore()
    for k in range(1, n):
        pl.semaphore_signal(barrier, inc=1, device_id=peer(k)[1], device_id_type=MESH)
    for k in range(1, ch):
        pl.semaphore_signal(barrier, inc=1, device_id={"ha": lax.rem(ih + k, ch)}, device_id_type=MESH)

    z = lax.broadcasted_iota(jnp.int32, (depth, 128), 0)

    def fill(x, carry):
        kvg[REACH + x, rim : rim + rows, : 2 * HD] = dot(tok[x], wkv[...], 1, 0).astype(jnp.bfloat16)
        for y in range(ny):
            live = jnp.right_shift(jnp.full((depth, 128), bits[x, y], jnp.int32), z) & 1
            kvg[REACH + x, rim + y * depth : rim + (y + 1) * depth, 2 * HD :] = (
                1.0 - live.astype(jnp.float32)
            ).astype(jnp.bfloat16)
        return carry

    lax.fori_loop(0, nx, fill, 0)

    def blank(where_x, where_r):
        shape = kvg.at[where_x, where_r, : 2 * HD].shape
        kvg[where_x, where_r, : 2 * HD] = jnp.zeros(shape, jnp.bfloat16)
        kvg[where_x, where_r, 2 * HD :] = jnp.ones(shape, jnp.bfloat16)

    xs_low, xs_high = slice(0, REACH), slice(REACH + nx, nx + 2 * REACH)
    rs_low, rs_mid, rs_high = slice(0, rim), slice(rim, rim + rows), slice(rim + rows, rows + 2 * rim)
    pl.when(ix == 0)(lambda: blank(xs_low, rs_mid))
    pl.when(ix == cx - 1)(lambda: blank(xs_high, rs_mid))
    pl.when(iy == 0)(lambda: blank(slice(None), rs_low))
    pl.when(iy == cy - 1)(lambda: blank(slice(None), rs_high))

    pl.semaphore_wait(barrier, n - 1 + ch - 1)
    swap(
        "gx", cx,
        send(kvg.at[REACH : 2 * REACH, rs_mid], kvg.at[xs_high, rs_mid], sem_h.at[0], sem_hr.at[0], {"gx": ix - 1}),
        send(kvg.at[nx : nx + REACH, rs_mid], kvg.at[xs_low, rs_mid], sem_h.at[1], sem_hr.at[1], {"gx": ix + 1}),
    )
    swap(
        "gy", cy,
        send(kvg.at[:, rim : 2 * rim], kvg.at[:, rs_high], sem_h.at[2], sem_hr.at[2], {"gy": iy - 1}),
        send(kvg.at[:, rows : rows + rim], kvg.at[:, rs_low], sem_h.at[3], sem_hr.at[3], {"gy": iy + 1}),
    )

    acc[...] = jnp.zeros_like(acc)
    wg[...] = jnp.zeros_like(wg)
    kx, kr = bx + 2 * REACH, (by + 2 * REACH) * depth
    qr = by * depth
    nq, nk = bx * qr, kx * kr
    across = ny // by

    def body(i, carry):
        x0 = (i // across) * bx
        r0 = pl.multiple_of(lax.rem(i, across) * qr, qr)
        mine = (pl.ds(x0, bx), pl.ds(r0, qr))
        wide = (pl.ds(x0, kx), pl.ds(r0, kr))
        tb = tok[mine].reshape(nq, -1)
        cb = cot[mine].reshape(nq, -1)
        q = (dot(tb, wq[...], 1, 0).astype(jnp.bfloat16).astype(jnp.float32) * scale).astype(jnp.bfloat16)
        u = dot(cb, wo[...], 1, 1).astype(jnp.bfloat16)
        keys = kvg[pl.ds(x0, kx), pl.ds(r0, kr), : 2 * HD].reshape(nk, 2 * HD)
        g1 = kvg[pl.ds(x0, kx), pl.ds(r0, kr), 2 * HD :].reshape(nk, 128).astype(jnp.float32)
        g1 = jnp.concatenate([g1] * (nq // 128), axis=1)
        s = jnp.where(table[...] > g1, dot(keys, q, 1, 1), -1e30)
        e = jnp.exp(s - jnp.max(s, axis=0, keepdims=True))
        p = (e * (1.0 / jnp.sum(e, axis=0, keepdims=True))).astype(jnp.bfloat16)
        o = dot(keys, p, 0, 0)
        r = jnp.sum(u.astype(jnp.float32).T * o, axis=0, keepdims=True)
        g = dot(keys, u, 1, 1)
        ds = (p.astype(jnp.float32) * (g - r)).astype(jnp.bfloat16)
        dq = dot(keys, ds, 0, 0) * scale
        dkv = dot(ds, q, 1, 0) + dot(p, u, 1, 0)
        acc[wide] += dkv.reshape(kx, kr, 2 * HD)
        wg[:HD] += dot(dq[:HD].astype(jnp.bfloat16), tb, 1, 0)
        wg[HD:] += dot(o[HD:].astype(jnp.bfloat16), cb, 1, 0)
        dq_all[mine] = dq.T.astype(jnp.bfloat16).reshape(bx, qr, 2 * HD)
        return carry

    lax.fori_loop(0, (nx // bx) * across, body, 0)

    sx[0] = acc[:REACH].astype(jnp.bfloat16)
    sx[1] = acc[REACH + nx :].astype(jnp.bfloat16)
    swap(
        "gx", cx,
        send(sx.at[0], rx.at[1], sem_h.at[4], sem_hr.at[4], {"gx": ix - 1}),
        send(sx.at[1], rx.at[0], sem_h.at[5], sem_hr.at[5], {"gx": ix + 1}),
    )
    cen[...] = acc[REACH : REACH + nx]

    @pl.when(ix > 0)
    def _():
        cen[:REACH] += rx[0].astype(jnp.float32)

    @pl.when(ix < cx - 1)
    def _():
        cen[nx - REACH :] += rx[1].astype(jnp.float32)

    sy[0] = cen[:, :rim].astype(jnp.bfloat16)
    sy[1] = cen[:, rim + rows :].astype(jnp.bfloat16)
    swap(
        "gy", cy,
        send(sy.at[0], ry.at[1], sem_h.at[6], sem_hr.at[6], {"gy": iy - 1}),
        send(sy.at[1], ry.at[0], sem_h.at[7], sem_hr.at[7], {"gy": iy + 1}),
    )

    @pl.when(iy > 0)
    def _():
        cen[:, rim : 2 * rim] += ry[0].astype(jnp.float32)

    @pl.when(iy < cy - 1)
    def _():
        cen[:, rows : rows + rim] += ry[1].astype(jnp.float32)

    dkv_all[...] = cen[:, rs_mid].astype(jnp.bfloat16)
    share = width // ch

    def product(j):
        cols = pl.ds(pl.multiple_of(j * share, 16), share)
        dkv = dkv_all[...].reshape(nx * rows, 2 * HD)
        dqs = dq_all[...].reshape(nx * rows, 2 * HD)
        return dot(wkv[cols, :], dkv, 1, 1) + dot(wq[cols, :], dqs, 1, 1)

    parts = []
    for k in range(1, ch):
        j = lax.rem(ih + k, ch)
        psend[k - 1] = product(j).astype(jnp.bfloat16)
        copy = send(psend.at[k - 1], precv.at[k - 1], sem_p.at[k - 1], sem_pr.at[k - 1], {"ha": j})
        copy.start()
        parts.append(copy)

    gsrc[: 2 * HD] = wg[...]
    gsrc[2 * HD :] = dot(
        dkv_all[...].reshape(nx * rows, 2 * HD), tok[...].reshape(nx * rows, width), 0, 0
    )
    piece = 4 * HD // n
    first = []
    for k in range(1, n):
        t, where = peer(k)
        src = gsrc.at[pl.ds(pl.multiple_of(t * piece, 8), piece)]
        copy = send(src, grecv.at[k - 1], sem_g.at[k - 1], sem_gr.at[k - 1], where)
        copy.start()
        first.append(copy)
    own[...] = product(ih)
    mine = pl.ds(pl.multiple_of(flat * piece, 8), piece)
    total = gsrc[mine]
    for k in range(1, n):
        first[k - 1].wait_recv()
        total += grecv[k - 1]
    gsum[mine] = total
    second = []
    for k in range(1, n):
        copy = send(gsum.at[mine], gsum.at[mine], sem_b.at[k - 1], sem_br.at[k - 1], peer(k)[1])
        copy.start()
        second.append(copy)
    for copy in first:
        copy.wait_send()
    for k in range(1, n):
        t = lax.rem(flat + n - k, n)
        other = gsum.at[pl.ds(pl.multiple_of(t * piece, 8), piece)]
        send(other, other, sem_b.at[k - 1], sem_br.at[k - 1], peer(k)[1]).wait_recv()
    for copy in second:
        copy.wait_send()
    norm = (n * nx * rows) ** (-0.5)
    everything = gsum[...] * norm
    output_out[...] = everything[HD : 2 * HD]
    input_out[...] = jnp.concatenate([everything[:HD], everything[2 * HD :]], axis=0).T
    for copy in parts:
        copy.wait()
    summed = own[...]
    for k in range(1, ch):
        summed += precv[k - 1].astype(jnp.float32)
    token_out[...] = summed.T.astype(jnp.bfloat16)


def shards(tokens, input_weight, output_weight, tissue_bits, cotangent):
    nx, ny, depth, width = tokens.shape
    rows, rim = ny * depth, REACH * depth
    sizes = tuple(lax.axis_size(a) for a in ("gx", "gy", "ha"))
    n, ch = sizes[0] * sizes[1], sizes[2]
    tok = tokens.reshape(nx, rows, width)
    cot = cotangent.reshape(nx, rows, width)
    wq = jnp.pad(input_weight[:, :HD], ((0, 0), (0, HD)))
    wkv = input_weight[:, HD:]
    wo = jnp.pad(output_weight, ((HD, 0), (0, 0)))
    bx, by = tile_of(nx), tile_of(ny)
    table = jnp.asarray(mask_table(bx, by, depth))
    px, pr = nx + 2 * REACH, rows + 2 * rim
    bf, f32, dma = jnp.bfloat16, jnp.float32, pltpu.SemaphoreType.DMA
    share = width // ch
    token_gradient, input_gradient, output_gradient = pl.pallas_call(
        functools.partial(kernel, sizes, depth, bx, by),
        out_shape=(
            jax.ShapeDtypeStruct((nx * rows, share), bf),
            jax.ShapeDtypeStruct((width, 3 * HD), f32),
            jax.ShapeDtypeStruct((HD, width), f32),
        ),
        in_specs=[VMEM] * 5 + [SMEM, VMEM],
        out_specs=(VMEM,) * 3,
        scratch_shapes=[
            pltpu.VMEM((px, pr, 4 * HD), bf),
            pltpu.VMEM((px, pr, 2 * HD), f32),
            pltpu.VMEM((2 * HD, width), f32),
            pltpu.VMEM((nx, rows, 2 * HD), bf),
            pltpu.VMEM((nx, pr, 2 * HD), f32),
            pltpu.VMEM((nx, rows, 2 * HD), bf),
            pltpu.VMEM((2, REACH, pr, 2 * HD), bf),
            pltpu.VMEM((2, REACH, pr, 2 * HD), bf),
            pltpu.VMEM((2, nx, rim, 2 * HD), bf),
            pltpu.VMEM((2, nx, rim, 2 * HD), bf),
            pltpu.VMEM((ch - 1, share, nx * rows), bf),
            pltpu.VMEM((ch - 1, share, nx * rows), bf),
            pltpu.VMEM((share, nx * rows), f32),
            pltpu.VMEM((4 * HD, width), f32),
            pltpu.VMEM((n - 1, 4 * HD // n, width), f32),
            pltpu.VMEM((4 * HD, width), f32),
            dma((8,)), dma((8,)),
            dma((ch - 1,)), dma((ch - 1,)),
            dma((n - 1,)), dma((n - 1,)),
            dma((n - 1,)), dma((n - 1,)),
        ],
        compiler_params=pltpu.CompilerParams(
            collective_id=0, has_side_effects=True, vmem_limit_bytes=56 * 1024 * 1024
        ),
        name="whole",
    )(tok, cot, wq, wkv, wo, tissue_bits, table)
    return token_gradient.reshape(nx, ny, depth, share), input_gradient, output_gradient


def solution(mesh):
    placed = (
        P("gx", "gy", None, None),
        P(None, "ha"),
        P("ha", None),
        P("gx", "gy"),
        P("gx", "gy", None, None),
    )
    return jax.shard_map(
        shards,
        mesh=mesh,
        in_specs=placed,
        out_specs=(P("gx", "gy", None, "ha"), P(None, "ha"), P("ha", None)),
        check_vma=False,
    )
```

time: 160 us -> 97.2 us (0.61); the launches traced: 157 us -> 96.9 us
  waiting for transfers between devices: 62.1 us -> 0 us
  Pallas kernels: 27.6 us -> 87.2 us
  starting transfers between devices: 20.8 us -> 0 us
  between operations: 15.8 us -> 0.66 us
  blocking collectives: 11 us -> 0 us
  local copies, waits for them, and re-layouts: 13.1 us -> 7.72 us
  other arithmetic: 5.05 us -> 1.31 us
  matrix products: 2.01 us -> 0 us
    pallas_call x2 -> x1, Pallas kernels: 27.6 us -> 87.2 us  [shards(): pl.pallas_call(functools.partial(kernel, sizes, depth, bx, by), out_shape...]
    psum x1 -> x0, waiting for transfers between devices: 53.5 us -> none  [shards(): summed = lax.psum(grads, ('gx', 'gy')).astype(jnp.float32) * count ** (-0.5)]
    ppermute x8 -> x0, starting transfers between devices: 20.7 us -> none  [shift(): return lax.ppermute(array, axis, pairs)]
    all_gather x1 -> x0, blocking collectives: 11 us -> none  [window_bits(): whole = lax.all_gather(tissue_bits, ('gx', 'gy'))]
    ppermute x8 -> x0, waiting for transfers between devices: 8.57 us -> none  [shift(): return lax.ppermute(array, axis, pairs)]
    unnamed x41 -> x7, local copies, waits for them, and re-layouts: 12.1 us -> 5.28 us
    another operation x1 -> x0, other arithmetic: 2.14 us -> none
    dot_general x1 -> x0, matrix products: 2.01 us -> none  [shards(): jnp.dot(tok.reshape(nx * rows, width), wkv, preferred_element_type=jnp.fl...]
  transfers between devices with their start and end apart: 10 -> 0, of which waited for: 6 -> 0; matrix products, arithmetic and copies ran while one was open for 3% -> 0% of each run, Pallas kernels for 0% -> 0%
where the time goes in v2:
time: 97.2 us; the launch traced here: 96.9 us
  Pallas kernels  87.2 us (90%)
  local copies, waits for them, and re-layouts  7.72 us (8%)
  other arithmetic  1.31 us (1%)
    pallas_call x1, Pallas kernels, shards(): pl.pallas_call(functools.partial(kernel, sizes, depth, bx, by), out_shape...  87.2 us
    unnamed x7, local copies, waits for them, and re-layouts  5.28 us

profile of v2, /device:TPU:9, one launch (start us, length us, event | category | flops | bytes accessed | tf_op | source)
XLA Modules:
  0.0 96.9 jit_solution(11891142454752891562)
XLA Ops:
  0.6 1.4 %pad.9.wo = bf16[128,384]{1,0:T(8,128)(2,1)} pad(bf16[64,384]{1,0:T(8,128)(2,1)} %param.8, bf16[]{:T(256)} %constant.6.clone.1), padding=64_0x0_0 | pad | bytes 147458 | tf_op jit(solution)/shard_map/jit(_pad)/pad | solution.py:264
  2.1 1.0 %fusion = (bf16[384,128]{0,1:T(8,128)(2,1)S(1)}, bf16[384,128]{0,1:T(8,128)(2,1)S(1)}) fusion(bf16[384,192]{0,1:T(8,128)(2,1)} %param.7), kind=kLoop, calls=%fused_computation.1 | loop fusion | bytes 393216 | tf_op jit(solution)/shard_map/slice | solution.py:263
  3.1 0.8 copy.13.wkv
  3.8 0.1 copy.12
  3.9 1.3 %broadcast_select_fusion.wq = bf16[384,128]{1,0:T(8,128)(2,1)} fusion(bf16[384,128]{1,0:T(8,128)(2,1)S(1)} %copy.12, pred[128]{0:T(512)(128)(4,1)} %constant.5.clone.1), kind=kLoop, calls=%fused_computation | loop fusion | flops 49152 | bytes 196736 | tf_op jit(solution)/shard_map/jit(_pad)/pad | solution.py:262
  5.3 87.2 %whole.1 = (bf16[2048,96]{1,0:T(8,128)(2,1)}, f32[384,192]{1,0:T(8,128)}, f32[64,384]{1,0:T(8,128)}) custom-call(bf16[8,256,384]{2,1,0:T(8,128)(2,1)} %bitcast.3, bf16[8,256,384]{2,1,0:T(8,128)(2,1)} %bitcast.4, bf16[384,128]{1,0:T(8,128)(2,1)} %broadcast_select_fusion.wq, bf16[384,128]{1,0:T(8,128)(2,1)} %copy.13.wkv, bf16[128,384]{1,0:T(8,128)(2,1)} %pad.9.wo, ...), custom_call_target="tpu_custom_call" | custom-call | tf_op jit(solution)/shard_map/whole/pallas_call | solution.py:270
  92.5 0.0 copy-start
  92.5 1.9 %copy.11 = f32[384,192]{0,1:T(8,128)} copy(f32[384,192]{1,0:T(8,128)} %get-tuple-element.10) | data formatting | bytes 589824
  94.4 1.9 %copy.16 = bf16[8,16,16,96]{3,2,1,0:T(8,128)(2,1)} copy(bf16[8,16,16,96]{3,2,1,0:T(8,128)(2,1)} %bitcast.5) | data formatting | bytes 786432
  96.3 0.0 copy-done
  96.3 0.6 copy.17
Async XLA Ops:
  92.5 3.8 %copy-start = (f32[64,384]{1,0:T(8,128)S(1)}, f32[64,384]{1,0:T(8,128)}, u32[]{:S(2)}) copy-start(f32[64,384]{1,0:T(8,128)} %get-tuple-element.19) | copy-start | bytes 294916

commit v3 on v2

--- a/solution.py
+++ b/solution.py
@@ -61,9 +61,9 @@
 
 
 def kernel(
-    sizes, depth, bx, by, tok, cot, wq, wkv, wo, bits, table,
+    sizes, depth, bx, by, tok, cot, weights, outer, bits, table,
     token_out, input_out, output_out,
-    kvg, acc, wg, dq_all, cen, dkv_all, sx, rx, sy, ry, psend, precv, own, gsrc, grecv, gsum,
+    wq, wkv, wo, kvg, acc, wg, dq_all, cen, dkv_all, sx, rx, sy, ry, psend, precv, own, gsrc, grecv, gsum,
     sem_h, sem_hr, sem_p, sem_pr, sem_g, sem_gr, sem_b, sem_br,
 ):
     cx, cy, ch = sizes
@@ -85,6 +85,12 @@
     for k in range(1, ch):
         pl.semaphore_signal(barrier, inc=1, device_id={"ha": lax.rem(ih + k, ch)}, device_id_type=MESH)
 
+    turned = weights[...].astype(jnp.float32)
+    blank_rows = jnp.zeros((HD, width), jnp.float32)
+    wq[...] = jnp.concatenate([turned[:HD], blank_rows], axis=0).T.astype(jnp.bfloat16)
+    wkv[...] = turned[HD:].T.astype(jnp.bfloat16)
+    wo[:HD] = blank_rows.astype(jnp.bfloat16)
+    wo[HD:] = outer[...]
     z = lax.broadcasted_iota(jnp.int32, (depth, 128), 0)
 
     def fill(x, carry):
@@ -156,7 +162,7 @@
         dq_all[mine] = dq.T.astype(jnp.bfloat16).reshape(bx, qr, 2 * HD)
         return carry
 
-    lax.fori_loop(0, (nx // bx) * across, body, 0)
+    lax.fori_loop(0, (nx // bx) * across, body, 0, unroll=2)
 
     sx[0] = acc[:REACH].astype(jnp.bfloat16)
     sx[1] = acc[REACH + nx :].astype(jnp.bfloat16)
@@ -243,7 +249,8 @@
     norm = (n * nx * rows) ** (-0.5)
     everything = gsum[...] * norm
     output_out[...] = everything[HD : 2 * HD]
-    input_out[...] = jnp.concatenate([everything[:HD], everything[2 * HD :]], axis=0).T
+    input_out[:HD] = everything[:HD]
+    input_out[HD:] = everything[2 * HD :]
     for copy in parts:
         copy.wait()
     summed = own[...]
@@ -259,9 +266,6 @@
     n, ch = sizes[0] * sizes[1], sizes[2]
     tok = tokens.reshape(nx, rows, width)
     cot = cotangent.reshape(nx, rows, width)
-    wq = jnp.pad(input_weight[:, :HD], ((0, 0), (0, HD)))
-    wkv = input_weight[:, HD:]
-    wo = jnp.pad(output_weight, ((HD, 0), (0, 0)))
     bx, by = tile_of(nx), tile_of(ny)
     table = jnp.asarray(mask_table(bx, by, depth))
     px, pr = nx + 2 * REACH, rows + 2 * rim
@@ -271,12 +275,15 @@
         functools.partial(kernel, sizes, depth, bx, by),
         out_shape=(
             jax.ShapeDtypeStruct((nx * rows, share), bf),
-            jax.ShapeDtypeStruct((width, 3 * HD), f32),
+            jax.ShapeDtypeStruct((3 * HD, width), f32),
             jax.ShapeDtypeStruct((HD, width), f32),
         ),
-        in_specs=[VMEM] * 5 + [SMEM, VMEM],
+        in_specs=[VMEM] * 4 + [SMEM, VMEM],
         out_specs=(VMEM,) * 3,
         scratch_shapes=[
+            pltpu.VMEM((width, 2 * HD), bf),
+            pltpu.VMEM((width, 2 * HD), bf),
+            pltpu.VMEM((2 * HD, width), bf),
             pltpu.VMEM((px, pr, 4 * HD), bf),
             pltpu.VMEM((px, pr, 2 * HD), f32),
             pltpu.VMEM((2 * HD, width), f32),
@@ -302,8 +309,8 @@
             collective_id=0, has_side_effects=True, vmem_limit_bytes=56 * 1024 * 1024
         ),
         name="whole",
-    )(tok, cot, wq, wkv, wo, tissue_bits, table)
-    return token_gradient.reshape(nx, ny, depth, share), input_gradient, output_gradient
+    )(tok, cot, input_weight.T, output_weight, tissue_bits, table)
+    return token_gradient.reshape(nx, ny, depth, share), input_gradient.T, output_gradient
 
 
 def solution(mesh):

time: 97.2 us -> 91.7 us (0.943)
  local copies, waits for them, and re-layouts: 7.72 us -> 4.24 us
  other arithmetic: 1.31 us -> 0 us
    pad x1 -> x0, local copies, waits for them, and re-layouts: 1.45 us -> none  [shards(): wo = jnp.pad(output_weight, ((HD, 0), (0, 0)))]
    pad x1 -> x0, other arithmetic: 1.31 us -> none  [shards(): wq = jnp.pad(input_weight[:, :HD], ((0, 0), (0, HD)))]
    unnamed x7 -> x5, local copies, waits for them, and re-layouts: 5.28 us -> 4.24 us
    slice x1 -> x0, local copies, waits for them, and re-layouts: 0.99 us -> none  [shards(): wkv = input_weight[:, HD:]]
where the time goes in v3:
time: 91.7 us; the launch traced here: 91.5 us
  Pallas kernels  86.6 us (94%)
  local copies, waits for them, and re-layouts  4.24 us (5%)
    pallas_call x1, Pallas kernels, shards(): pl.pallas_call(functools.partial(kernel, sizes, depth, bx, by), out_shape...  86.6 us
    unnamed x5, local copies, waits for them, and re-layouts  4.24 us

profile of v3, /device:TPU:9, one launch (start us, length us, event | category | flops | bytes accessed | tf_op | source)
XLA Modules:
  0.0 91.5 jit_solution(11985980614730582558)
XLA Ops:
  0.6 86.6 %whole.1 = (bf16[2048,96]{1,0:T(8,128)(2,1)}, f32[192,384]{1,0:T(8,128)}, f32[64,384]{1,0:T(8,128)}) custom-call(bf16[8,256,384]{2,1,0:T(8,128)(2,1)} %bitcast.5, bf16[8,256,384]{2,1,0:T(8,128)(2,1)} %bitcast.6, bf16[192,384]{1,0:T(8,128)(2,1)} %bitcast.9, bf16[64,384]{1,0:T(8,128)(2,1)} %outer.1, s32[8,16]{1,0:T(8,128)} %bits.1, ...), custom_call_target="tpu_custom_call" | custom-call | tf_op jit(solution)/shard_map/whole/pallas_call | solution.py:274
  87.2 0.0 copy-start
  87.3 1.9 %copy.12 = bf16[8,16,16,96]{3,2,1,0:T(8,128)(2,1)} copy(bf16[8,16,16,96]{3,2,1,0:T(8,128)(2,1)} %bitcast.7) | data formatting | bytes 786432
  89.2 1.7 %copy.13 = f32[384,192]{0,1:T(8,128)} copy(f32[384,192]{0,1:T(8,128)} %bitcast.8) | data formatting | bytes 589824
  90.9 0.0 copy-done
  90.9 0.6 copy.14
Async XLA Ops:
  87.2 3.6 %copy-start = (f32[64,384]{1,0:T(8,128)S(1)}, f32[64,384]{1,0:T(8,128)}, u32[]{:S(2)}) copy-start(f32[64,384]{1,0:T(8,128)} %get-tuple-element.14) | copy-start | bytes 294916

commit v4 on v3

--- a/solution.py
+++ b/solution.py
@@ -200,19 +200,27 @@
     dkv_all[...] = cen[:, rs_mid].astype(jnp.bfloat16)
     share = width // ch
 
-    def product(j):
+    half = nx // 2
+    halves = (0, 1)
+    near = ih + 1 - 2 * lax.rem(ih, 2)
+    far, corner = lax.rem(ih + 2, ch), lax.rem(near + 2, ch)
+
+    def product(j, h):
         cols = pl.ds(pl.multiple_of(j * share, 16), share)
-        dkv = dkv_all[...].reshape(nx * rows, 2 * HD)
-        dqs = dq_all[...].reshape(nx * rows, 2 * HD)
+        dkv = dkv_all[h * half : (h + 1) * half].reshape(half * rows, 2 * HD)
+        dqs = dq_all[h * half : (h + 1) * half].reshape(half * rows, 2 * HD)
         return dot(wkv[cols, :], dkv, 1, 1) + dot(wq[cols, :], dqs, 1, 1)
 
-    parts = []
-    for k in range(1, ch):
-        j = lax.rem(ih + k, ch)
-        psend[k - 1] = product(j).astype(jnp.bfloat16)
-        copy = send(psend.at[k - 1], precv.at[k - 1], sem_p.at[k - 1], sem_pr.at[k - 1], {"ha": j})
-        copy.start()
-        parts.append(copy)
+    def hop(slot, h, where):
+        i = 2 * slot + h
+        return send(psend.at[i], precv.at[i], sem_p.at[i], sem_pr.at[i], {"ha": where})
+
+    relay = [hop(0, h, near) for h in halves]
+    close = [hop(1, h, near) for h in halves]
+    long = [hop(2, h, far) for h in halves]
+    for h in halves:
+        psend[h] = product(corner, h).astype(jnp.bfloat16)
+        relay[h].start()
 
     gsrc[: 2 * HD] = wg[...]
     gsrc[2 * HD :] = dot(
@@ -226,7 +234,16 @@
         copy = send(src, grecv.at[k - 1], sem_g.at[k - 1], sem_gr.at[k - 1], where)
         copy.start()
         first.append(copy)
-    own[...] = product(ih)
+    for h in halves:
+        psend[2 + h] = product(near, h).astype(jnp.bfloat16)
+    for h in halves:
+        mixed = product(far, h)
+        relay[h].wait_recv()
+        psend[4 + h] = (mixed + precv[h].astype(jnp.float32)).astype(jnp.bfloat16)
+        long[h].start()
+    for h in halves:
+        close[h].start()
+        own[h] = product(ih, h)
     mine = pl.ds(pl.multiple_of(flat * piece, 8), piece)
     total = gsrc[mine]
     for k in range(1, n):
@@ -251,12 +268,13 @@
     output_out[...] = everything[HD : 2 * HD]
     input_out[:HD] = everything[:HD]
     input_out[HD:] = everything[2 * HD :]
-    for copy in parts:
-        copy.wait()
-    summed = own[...]
-    for k in range(1, ch):
-        summed += precv[k - 1].astype(jnp.float32)
-    token_out[...] = summed.T.astype(jnp.bfloat16)
+    for h in halves:
+        long[h].wait_recv()
+        close[h].wait_recv()
+        summed = own[h] + precv[2 + h].astype(jnp.float32) + precv[4 + h].astype(jnp.float32)
+        token_out[h * half * rows : (h + 1) * half * rows] = summed.T.astype(jnp.bfloat16)
+    for copy in relay + close + long:
+        copy.wait_send()
 
 
 def shards(tokens, input_weight, output_weight, tissue_bits, cotangent):
@@ -294,14 +312,14 @@
             pltpu.VMEM((2, REACH, pr, 2 * HD), bf),
             pltpu.VMEM((2, nx, rim, 2 * HD), bf),
             pltpu.VMEM((2, nx, rim, 2 * HD), bf),
-            pltpu.VMEM((ch - 1, share, nx * rows), bf),
-            pltpu.VMEM((ch - 1, share, nx * rows), bf),
-            pltpu.VMEM((share, nx * rows), f32),
+            pltpu.VMEM((6, share, nx * rows // 2), bf),
+            pltpu.VMEM((6, share, nx * rows // 2), bf),
+            pltpu.VMEM((2, share, nx * rows // 2), f32),
             pltpu.VMEM((4 * HD, width), f32),
             pltpu.VMEM((n - 1, 4 * HD // n, width), f32),
             pltpu.VMEM((4 * HD, width), f32),
             dma((8,)), dma((8,)),
-            dma((ch - 1,)), dma((ch - 1,)),
+            dma((6,)), dma((6,)),
             dma((n - 1,)), dma((n - 1,)),
             dma((n - 1,)), dma((n - 1,)),
         ],

time: 91.7 us -> 83.9 us (0.915)
  Pallas kernels: 86.6 us -> 77.9 us
    pallas_call x1, Pallas kernels: 86.6 us -> 77.9 us  [shards(): pl.pallas_call(functools.partial(kernel, sizes, depth, bx, by), out_shape...]
where the time goes in v4:
time: 83.9 us; the launch traced here: 82.8 us
  Pallas kernels  77.9 us (93%)
  local copies, waits for them, and re-layouts  4.24 us (5%)
    pallas_call x1, Pallas kernels, shards(): pl.pallas_call(functools.partial(kernel, sizes, depth, bx, by), out_shape...  77.9 us
    unnamed x5, local copies, waits for them, and re-layouts  4.24 us

profile of v4, /device:TPU:9, one launch (start us, length us, event | category | flops | bytes accessed | tf_op | source)
XLA Modules:
  0.0 82.8 jit_solution(4731234035837021354)
XLA Ops:
  0.6 77.9 %whole.1 = (bf16[2048,96]{1,0:T(8,128)(2,1)}, f32[192,384]{1,0:T(8,128)}, f32[64,384]{1,0:T(8,128)}) custom-call(bf16[8,256,384]{2,1,0:T(8,128)(2,1)} %bitcast.5, bf16[8,256,384]{2,1,0:T(8,128)(2,1)} %bitcast.6, bf16[192,384]{1,0:T(8,128)(2,1)} %bitcast.9, bf16[64,384]{1,0:T(8,128)(2,1)} %outer.1, s32[8,16]{1,0:T(8,128)} %bits.1, ...), custom_call_target="tpu_custom_call" | custom-call | tf_op jit(solution)/shard_map/whole/pallas_call | solution.py:292
  78.6 0.0 copy-start
  78.6 1.9 %copy.12 = bf16[8,16,16,96]{3,2,1,0:T(8,128)(2,1)} copy(bf16[8,16,16,96]{3,2,1,0:T(8,128)(2,1)} %bitcast.7) | data formatting | bytes 786432
  80.5 1.7 %copy.13 = f32[384,192]{0,1:T(8,128)} copy(f32[384,192]{0,1:T(8,128)} %bitcast.8) | data formatting | bytes 589824
  82.2 0.0 copy-done
  82.2 0.6 copy.14
Async XLA Ops:
  78.6 3.6 %copy-start = (f32[64,384]{1,0:T(8,128)S(1)}, f32[64,384]{1,0:T(8,128)}, u32[]{:S(2)}) copy-start(f32[64,384]{1,0:T(8,128)} %get-tuple-element.14) | copy-start | bytes 294916

commit v5 on v4

--- a/solution.py
+++ b/solution.py
@@ -200,8 +200,9 @@
     dkv_all[...] = cen[:, rs_mid].astype(jnp.bfloat16)
     share = width // ch
 
-    half = nx // 2
-    halves = (0, 1)
+    pieces = psend.shape[0] // 3
+    half = nx // pieces
+    halves = range(pieces)
     near = ih + 1 - 2 * lax.rem(ih, 2)
     far, corner = lax.rem(ih + 2, ch), lax.rem(near + 2, ch)
 
@@ -212,7 +213,7 @@
         return dot(wkv[cols, :], dkv, 1, 1) + dot(wq[cols, :], dqs, 1, 1)
 
     def hop(slot, h, where):
-        i = 2 * slot + h
+        i = pieces * slot + h
         return send(psend.at[i], precv.at[i], sem_p.at[i], sem_pr.at[i], {"ha": where})
 
     relay = [hop(0, h, near) for h in halves]
@@ -235,11 +236,11 @@
         copy.start()
         first.append(copy)
     for h in halves:
-        psend[2 + h] = product(near, h).astype(jnp.bfloat16)
+        psend[pieces + h] = product(near, h).astype(jnp.bfloat16)
     for h in halves:
         mixed = product(far, h)
         relay[h].wait_recv()
-        psend[4 + h] = (mixed + precv[h].astype(jnp.float32)).astype(jnp.bfloat16)
+        psend[2 * pieces + h] = (mixed + precv[h].astype(jnp.float32)).astype(jnp.bfloat16)
         long[h].start()
     for h in halves:
         close[h].start()
@@ -271,7 +272,7 @@
     for h in halves:
         long[h].wait_recv()
         close[h].wait_recv()
-        summed = own[h] + precv[2 + h].astype(jnp.float32) + precv[4 + h].astype(jnp.float32)
+        summed = own[h] + precv[pieces + h].astype(jnp.float32) + precv[2 * pieces + h].astype(jnp.float32)
         token_out[h * half * rows : (h + 1) * half * rows] = summed.T.astype(jnp.bfloat16)
     for copy in relay + close + long:
         copy.wait_send()
@@ -289,6 +290,7 @@
     px, pr = nx + 2 * REACH, rows + 2 * rim
     bf, f32, dma = jnp.bfloat16, jnp.float32, pltpu.SemaphoreType.DMA
     share = width // ch
+    pieces = 4 if nx % 4 == 0 else 1
     token_gradient, input_gradient, output_gradient = pl.pallas_call(
         functools.partial(kernel, sizes, depth, bx, by),
         out_shape=(
@@ -312,14 +314,14 @@
             pltpu.VMEM((2, REACH, pr, 2 * HD), bf),
             pltpu.VMEM((2, nx, rim, 2 * HD), bf),
             pltpu.VMEM((2, nx, rim, 2 * HD), bf),
-            pltpu.VMEM((6, share, nx * rows // 2), bf),
-            pltpu.VMEM((6, share, nx * rows // 2), bf),
-            pltpu.VMEM((2, share, nx * rows // 2), f32),
+            pltpu.VMEM((3 * pieces, share, nx * rows // pieces), bf),
+            pltpu.VMEM((3 * pieces, share, nx * rows // pieces), bf),
+            pltpu.VMEM((pieces, share, nx * rows // pieces), f32),
             pltpu.VMEM((4 * HD, width), f32),
             pltpu.VMEM((n - 1, 4 * HD // n, width), f32),
             pltpu.VMEM((4 * HD, width), f32),
             dma((8,)), dma((8,)),
-            dma((6,)), dma((6,)),
+            dma((3 * pieces,)), dma((3 * pieces,)),
             dma((n - 1,)), dma((n - 1,)),
             dma((n - 1,)), dma((n - 1,)),
         ],

time: 83.9 us -> 83.9 us (level)
  no operation moved by 1% of the time
where the time goes in v5:
time: 83.9 us; the launch traced here: 82.8 us
  Pallas kernels  77.9 us (93%)
  local copies, waits for them, and re-layouts  4.24 us (5%)
    pallas_call x1, Pallas kernels, shards(): pl.pallas_call(functools.partial(kernel, sizes, depth, bx, by), out_shape...  77.9 us
    unnamed x5, local copies, waits for them, and re-layouts  4.24 us

profile of v5, /device:TPU:9, one launch (start us, length us, event | category | flops | bytes accessed | tf_op | source)
XLA Modules:
  0.0 82.8 jit_solution(3168994595097683)
XLA Ops:
  0.6 77.9 %whole.1 = (bf16[2048,96]{1,0:T(8,128)(2,1)}, f32[192,384]{1,0:T(8,128)}, f32[64,384]{1,0:T(8,128)}) custom-call(bf16[8,256,384]{2,1,0:T(8,128)(2,1)} %bitcast.5, bf16[8,256,384]{2,1,0:T(8,128)(2,1)} %bitcast.6, bf16[192,384]{1,0:T(8,128)(2,1)} %bitcast.9, bf16[64,384]{1,0:T(8,128)(2,1)} %outer.1, s32[8,16]{1,0:T(8,128)} %bits.1, ...), custom_call_target="tpu_custom_call" | custom-call | tf_op jit(solution)/shard_map/whole/pallas_call | solution.py:294
  78.6 0.0 copy-start
  78.6 1.9 %copy.12 = bf16[8,16,16,96]{3,2,1,0:T(8,128)(2,1)} copy(bf16[8,16,16,96]{3,2,1,0:T(8,128)(2,1)} %bitcast.7) | data formatting | bytes 786432
  80.5 1.7 %copy.13 = f32[384,192]{0,1:T(8,128)} copy(f32[384,192]{0,1:T(8,128)} %bitcast.8) | data formatting | bytes 589824
  82.2 0.0 copy-done
  82.2 0.6 copy.14
Async XLA Ops:
  78.6 3.6 %copy-start = (f32[64,384]{1,0:T(8,128)S(1)}, f32[64,384]{1,0:T(8,128)}, u32[]{:S(2)}) copy-start(f32[64,384]{1,0:T(8,128)} %get-tuple-element.14) | copy-start | bytes 294916
